TPU v7x, 32 devices: a whole 2x2x4 slice. The times are simulated.
32 devices in a mesh: lat: 16 (over z, y, core), lev: 2 (over x).
Axes of the slice: x: 2, y: 2, z: 4, core: 2. Of those that a mesh axis runs over, the one named last changes fastest.
Arguments:
- spectral: bfloat16 [2, 512, 512, 128], P(None, 'lat', None, 'lev'), may hold values from -6 to 6
- legendre: bfloat16 [512, 512, 512], P('lat'), may hold values from -0.25 to 0.25
- gauss_weights: float32 [512], replicated, may hold values from 0.5 to 2
- w_first: bfloat16 [128, 256], replicated, may hold values from -0.5 to 0.5
- w_second: bfloat16 [256, 256], replicated, may hold values from -0.375 to 0.375
- w_third: bfloat16 [256, 128], replicated, may hold values from -0.375 to 0.375
- cotangent: bfloat16 [512, 1024, 128], P(('lat', 'lev')), may hold values from -6 to 6
Outputs:
- spectral_tendency: float32 [2, 512, 512, 128], P(None, 'lat', None, 'lev')
- grad_first: float32 [128, 256], replicated
- grad_second: float32 [256, 256], replicated
- grad_third: float32 [256, 128], replicated
All inputs are finite; a program needn't handle non-finite values.
Results may differ from a plain program's by a relative error of at most 0.0083.
Values may be sent and summed in bfloat16 or wider, within the bound.
No kernel may reach another device: no remote copies, remote signals or barrier semaphores. Data moves between devices by JAX's collectives and lax.ppermute only.
A program may use at most 192 MiB of HBM per device.

v0:
```python
import math

import jax
import jax.numpy as jnp
from jax import lax
from jax.sharding import PartitionSpec as P

WAVES = 512
NDEG = 512
NLAT = 512
NLON = 1024


def make_basis():
    waves = jnp.arange(WAVES, dtype=jnp.int32)
    places = jnp.arange(NLON, dtype=jnp.int32)
    phase = waves[:, None] * places[None, :] % NLON
    angle = phase.astype(jnp.float32) * (2.0 * math.pi / NLON)
    factor = 1.0 / math.sqrt(NLON)
    table = jnp.concatenate([jnp.cos(angle) * factor, -jnp.sin(angle) * factor], axis=0)
    return table.astype(jnp.bfloat16).reshape(2, WAVES, NLON)


def silu_slope(value):
    sig = jax.nn.sigmoid(value)
    return sig * (1.0 + value * (1.0 - sig))


def to_grid(coeffs, basis):
    return jnp.einsum("rmlf,rmo->lfo", coeffs, basis, preferred_element_type=jnp.float32).astype(
        jnp.bfloat16
    )


def to_waves(values, basis):
    return jnp.einsum("rmo,lof->rmlf", basis, values, preferred_element_type=jnp.float32).astype(
        jnp.bfloat16
    )


def shards(spectral, legendre, gauss_weights, w_first, w_second, w_third, cotangent):
    own_waves = legendre.shape[0]
    first_wave = lax.axis_index("lat") * own_waves
    wave_rows = first_wave + jnp.arange(own_waves, dtype=jnp.int32)
    keep = wave_rows[:, None] <= jnp.arange(NDEG, dtype=jnp.int32)[None, :]
    masked = jnp.where(keep[:, :, None], legendre, jnp.zeros((), jnp.bfloat16))
    basis = make_basis()
    fourier = jnp.einsum(
        "mnl,rmnf->rmlf", masked, spectral, preferred_element_type=jnp.float32
    ).astype(jnp.bfloat16)
    bands = lax.all_to_all(fourier, "lat", split_axis=2, concat_axis=1, tiled=True)
    grid_part = to_grid(bands, basis)
    grid = lax.all_to_all(grid_part, "lev", split_axis=0, concat_axis=1, tiled=True)
    factor = 1.0 / math.sqrt(NLAT * NLON)
    act_one = jnp.einsum("lfo,fh->loh", grid, w_first, preferred_element_type=jnp.float32)
    out_one = jax.nn.silu(act_one).astype(jnp.bfloat16)
    act_two = jnp.einsum("loh,hk->lok", out_one, w_second, preferred_element_type=jnp.float32)
    out_two = jax.nn.silu(act_two).astype(jnp.bfloat16)
    tend = jnp.einsum("lok,kf->lof", out_two, w_third, preferred_element_type=jnp.float32).astype(
        jnp.bfloat16
    )
    part_third = jnp.einsum("lok,lof->kf", out_two, cotangent, preferred_element_type=jnp.float32)
    delta_two = (
        jnp.einsum("lof,kf->lok", cotangent, w_third, preferred_element_type=jnp.float32)
        * silu_slope(act_two)
    ).astype(jnp.bfloat16)
    part_second = jnp.einsum("loh,lok->hk", out_one, delta_two, preferred_element_type=jnp.float32)
    delta_one = (
        jnp.einsum("lok,hk->loh", delta_two, w_second, preferred_element_type=jnp.float32)
        * silu_slope(act_one)
    ).astype(jnp.bfloat16)
    part_first = jnp.einsum("lfo,loh->fh", grid, delta_one, preferred_element_type=jnp.float32)
    total_first, total_second, total_third = lax.psum(
        (part_first, part_second, part_third), ("lat", "lev")
    )
    grad_first = total_first * factor
    grad_second = total_second * factor
    grad_third = total_third * factor
    levels_back = lax.all_to_all(tend, "lev", split_axis=2, concat_axis=0, tiled=True)
    back_part = to_waves(levels_back, basis)
    owned = lax.all_to_all(back_part, "lat", split_axis=1, concat_axis=2, tiled=True)
    weighted = (masked.astype(jnp.float32) * gauss_weights[None, None, :]).astype(jnp.bfloat16)
    spectral_tendency = jnp.einsum(
        "mnl,rmlf->rmnf", weighted, owned, preferred_element_type=jnp.float32
    )
    return (spectral_tendency, grad_first, grad_second, grad_third)


def solution(mesh):
    in_specs = (
        P(None, "lat", None, "lev"),
        P("lat", None, None),
        P(),
        P(),
        P(),
        P(),
        P(("lat", "lev"), None, None),
    )
    out_specs = (P(None, "lat", None, "lev"), P(), P(), P())
    return jax.shard_map(shards, mesh=mesh, in_specs=in_specs, out_specs=out_specs, check_vma=False)
```

profile of v0, /device:TPU:0, one launch (start us, length us, event | category | flops | bytes accessed | tf_op | source)
XLA Modules:
  0.0 620.3 jit_solution(12796918349966045962)
XLA Ops:
  7.2 0.0 copy-start
  7.2 0.1 iota_compare_fusion
  7.3 0.0 copy-start.6
  7.3 0.6 copy-done.6
  7.9 10.1 %convert_bitcast_fusion = bf16[2,32,512,64]{2,3,0,1:T(8,128)(2,1)} fusion(bf16[2,32,512,64]{2,3,1,0:T(8,128)(2,1)} %param.7, bf16[32,512,512]{2,1,0:T(8,128)(2,1)} %param.8, pred[32,512]{1,0:T(8,128)(4,1)S(1)} %iota_compare_fusion), kind=kOutput, calls=%fused_computation.21 | convolution fusion | flops 2157969408 | bytes 25182208 | tf_op jit(solution)/shard_map/mnl,rmnf->rmlf/dot_general | solution.py:48
  18.0 18.6 %copy.35 = bf16[2,32,512,64]{3,0,1,2:T(2,128)(2,1)} copy(bf16[2,32,512,64]{2,3,0,1:T(8,128)(2,1)} %convert_bitcast_fusion) | data formatting | bytes 8388608 | tf_op jit(solution)/shard_map/convert_element_type | solution.py:50
  36.6 14.0 %reshape.54 = bf16[16,2,65536]{2,1,0:T(2,128)(2,1)} reshape(bf16[512,32,2,64]{3,2,1,0:T(2,128)(2,1)} %bitcast.86) | data formatting | bytes 8388608
  50.6 7.4 %all-to-all-start = ((bf16[16,2,65536]{2,1,0:T(2,128)(2,1)}), bf16[16,2,65536]{2,1,0:T(2,128)(2,1)}, u32[]{:S(2)}, u32[]{:S(2)}) async-start(bf16[16,2,65536]{2,1,0:T(2,128)(2,1)} %reshape.54), calls=%async_computation | async-start | bytes 8388608 | tf_op jit(solution)/shard_map/all_to_all | solution.py:51
  58.1 8.6 %negate_multiply_fusion = (bf16[512,1024]{1,0:T(8,128)(2,1)S(1)}, bf16[512,1024]{1,0:T(8,128)(2,1)S(1)}) fusion(), kind=kLoop, calls=%fused_computation.32 | loop fusion | flops 9961472 | bytes 2097152 | tf_op jit(solution)/shard_map/mul | solution.py:20
  66.6 0.2 maximum_convert_fusion
  66.8 68.9 %all-to-all-done = bf16[16,2,65536]{2,1,0:T(2,128)(2,1)} async-done(((bf16[16,2,65536]{2,1,0:T(2,128)(2,1)}), bf16[16,2,65536]{2,1,0:T(2,128)(2,1)}, u32[]{:S(2)}, u32[]{:S(2)}) %all-to-all-start) | async-done | bytes 4194336 | tf_op jit(solution)/shard_map/all_to_all | solution.py:51
  135.7 13.6 %reshape.55 = bf16[512,32,2,64]{3,2,1,0:T(2,128)(2,1)} reshape(bf16[16,2,65536]{2,1,0:T(2,128)(2,1)} %all-to-all-done) | data formatting | bytes 8388608
  149.3 12.0 %copy.36 = bf16[2,32,512,64]{3,2,1,0:T(8,128)(2,1)} copy(bf16[2,32,512,64]{3,0,1,2:T(2,128)(2,1)} %bitcast.88) | data formatting | bytes 8388608 | tf_op jit(solution)/shard_map/all_to_all | solution.py:51
  161.4 9.3 %copy.37 = bf16[2,16,32,32,64]{4,3,2,1,0:T(8,128)(2,1)} copy(bf16[2,16,32,32,64]{4,3,1,2,0:T(8,128)(2,1)} %bitcast.89) | data formatting | bytes 8388608 | tf_op jit(solution)/shard_map/all_to_all | solution.py:51
  170.6 15.5 %bitcast_convert_fusion = bf16[32,64,1024]{2,1,0:T(8,128)(2,1)S(1)} fusion(bf16[2,512,1024,1]{2,1,0,3:T(8,128)(2,1)S(1)} %bitcast.93, bf16[2,512,32,64]{3,2,1,0:T(8,128)(2,1)} %bitcast.85), kind=kOutput, calls=%fused_computation.14 | convolution fusion | flops 4297064448 | bytes 10485760 | tf_op jit(solution)/shard_map/rmlf,rmo->lfo/dot_general | solution.py:30
  186.1 0.0 copy-start.8
  186.1 51.4 %all_to_all.72 = bf16[32,64,1024]{2,1,0:T(8,128)(2,1)S(1)} all-to-all(bf16[32,64,1024]{2,1,0:T(8,128)(2,1)S(1)} %bitcast_convert_fusion), channel_id=1, replica_groups=mesh['lat'=16,'lev'=2] {'lev'}, dimensions={0} | all-to-all | bytes 8388608 | tf_op jit(solution)/shard_map/all_to_all | solution.py:53
  237.5 0.4 copy.39
  238.0 0.0 copy-start.4
  238.0 0.0 copy-done.8
  238.0 8.1 %multiply_convert_fusion.4 = (bf16[16,1024,256]{2,1,0:T(8,128)(2,1)S(1)}, f32[16,1024,256]{2,1,0:T(8,128)}) fusion(bf16[16,128,1024]{2,1,0:T(8,128)(2,1)S(1)} %bitcast.95, bf16[128,256]{1,0:T(8,128)(2,1)S(1)} %copy-done.8), kind=kOutput, calls=%fused_computation.10 | convolution fusion | flops 1094713344 | bytes 29425664 | tf_op jit(solution)/shard_map/lfo,fh->loh/dot_general | solution.py:55
  246.1 0.0 copy-done.4
  246.1 0.0 copy-start.2
  246.1 0.0 copy-done
  246.1 0.0 copy-start.5
  246.1 8.2 %multiply_convert_fusion.3 = (bf16[16,1024,256]{2,1,0:T(8,128)(2,1)S(1)}, f32[16,1024,256]{2,1,0:T(8,128)}) fusion(bf16[16,1024,256]{2,1,0:T(8,128)(2,1)S(1)} %get-tuple-element.19, bf16[256,256]{1,0:T(8,128)(2,1)S(1)} %copy-done), kind=kOutput, calls=%fused_computation.8 | convolution fusion | flops 2168455168 | bytes 33685504 | tf_op jit(solution)/shard_map/loh,hk->lok/dot_general | solution.py:57
  254.3 0.0 copy-done.2
  254.3 0.0 copy-start.1
  254.3 3.4 copy-done.1
  257.7 0.0 copy-done.5
  257.7 4.4 convolution_convert_fusion.1
  262.1 6.8 %copy.41 = bf16[16,1024,128]{1,0,2:T(8,128)(2,1)} copy(bf16[16,1024,128]{2,1,0:T(8,128)(2,1)} %convolution_convert_fusion.1) | data formatting | bytes 8388608 | tf_op jit(solution)/shard_map/convert_element_type | solution.py:59
  269.0 5.7 all-to-all-start.2
  274.7 7.6 %convolution_bitcast_fusion.1 = f32[256,128]{1,0:T(8,128)} fusion(bf16[16,1024,256]{2,1,0:T(8,128)(2,1)} %copy-done.1, bf16[16,1024,128]{2,1,0:T(8,128)(2,1)} %param.13), kind=kOutput, calls=%fused_computation.39 | convolution fusion | flops 1073741824 | bytes 12713984 | tf_op jit(solution)/shard_map/lok,lof->kf/dot_general | solution.py:62
  282.3 40.1 %all-to-all-done.2 = bf16[16,1024,128]{1,0,2:T(8,128)(2,1)} async-done(((bf16[16,1024,128]{1,0,2:T(8,128)(2,1)}), bf16[16,1024,128]{1,0,2:T(8,128)(2,1)}, u32[]{:S(2)}, u32[]{:S(2)}) %all-to-all-start.2) | async-done | bytes 4194336 | tf_op jit(solution)/shard_map/all_to_all | solution.py:79
  322.4 4.5 copy.43
  326.9 6.1 convolution_convert_fusion
  333.0 12.9 %copy.44 = bf16[2,512,32,64]{3,2,0,1:T(8,128)(2,1)} copy(bf16[2,512,32,64]{1,3,2,0:T(8,128)(2,1)} %convolution_convert_fusion) | data formatting | bytes 8388608 | tf_op jit(solution)/shard_map/convert_element_type | solution.py:36
  346.0 14.0 %reshape.56 = bf16[16,2,65536]{2,1,0:T(2,128)(2,1)} reshape(bf16[512,2,32,64]{3,2,1,0:T(8,128)(2,1)} %bitcast.87) | data formatting | bytes 8388608
  359.9 18.8 %all-to-all-start.3 = ((bf16[16,2,65536]{2,1,0:T(2,128)(2,1)}), bf16[16,2,65536]{2,1,0:T(2,128)(2,1)}, u32[]{:S(2)}, u32[]{:S(2)}) async-start(bf16[16,2,65536]{2,1,0:T(2,128)(2,1)} %reshape.56), calls=%async_computation.3 | async-start | bytes 8388608 | tf_op jit(solution)/shard_map/all_to_all | solution.py:81
  378.7 0.3 all-reduce.3.cloned.1.call-start
  379.0 11.7 %multiply_convert_fusion.2 = bf16[16,1024,256]{2,1,0:T(8,128)(2,1)S(1)} fusion(f32[16,1024,256]{2,1,0:T(8,128)} %get-tuple-element.22, bf16[16,1024,128]{2,1,0:T(8,128)(2,1)} %param.13, bf16[256,128]{1,0:T(8,128)(2,1)S(1)} %copy-done.5), kind=kOutput, calls=%fused_computation.6 | convolution fusion | flops 1111490560 | bytes 29425664 | tf_op jit(solution)/shard_map/lof,kf->lok/dot_general | solution.py:64
  390.6 0.0 copy-start.3
  390.7 9.5 %convolution_bitcast_fusion = f32[256,256]{1,0:T(8,128)} fusion(bf16[16,1024,256]{2,1,0:T(8,128)(2,1)} %copy-done.2, bf16[16,1024,256]{2,1,0:T(8,128)(2,1)S(1)} %multiply_convert_fusion.2), kind=kOutput, calls=%fused_computation.37 | convolution fusion | flops 2147483648 | bytes 17039360 | tf_op jit(solution)/shard_map/loh,lok->hk/dot_general | solution.py:67
  400.2 0.0 copy-done.3
  400.2 13.8 %fusion.30 = f32[128,256]{1,0:T(8,128)} fusion(bf16[16,128,1024]{2,1,0:T(8,128)(2,1)} %bitcast.96, f32[16,1024,256]{2,1,0:T(8,128)} %get-tuple-element.20, bf16[16,1024,256]{2,1,0:T(8,128)(2,1)} %copy-done.3, bf16[256,256]{1,0:T(8,128)(2,1)S(1)} %copy-done), kind=kOutput, calls=%fused_computation.38 | convolution fusion | flops 3258974208 | bytes 29622272 | tf_op jit(solution)/shard_map/lfo,loh->fh/dot_general | solution.py:72
  414.0 0.0 all-reduce.3.cloned.1.call-update
  414.0 154.2 %all-reduce.3.cloned.1.call-done = (f32[128,256]{1,0:T(8,128)}, f32[256,256]{1,0:T(8,128)}, f32[256,128]{1,0:T(8,128)}) async-done(((f32[128,256]{1,0:T(8,128)}, f32[256,256]{1,0:T(8,128)}, f32[256,128]{1,0:T(8,128)}), (f32[128,256]{1,0:T(8,128)}, f32[256,256]{1,0:T(8,128)}, f32[256,128]{1,0:T(8,128)})) %all-reduce.3.cloned.1.call-update) | async-done | bytes 524304 | tf_op jit(solution)/shard_map/psum | solution.py:73
  568.2 1.6 broadcast_multiply_fusion.2
  569.8 1.6 broadcast_multiply_fusion.1
  571.3 1.7 broadcast_multiply_fusion
  573.0 0.0 all-to-all-done.3
  573.0 13.6 %reshape.57 = bf16[512,2,32,64]{3,2,1,0:T(8,128)(2,1)} reshape(bf16[16,2,65536]{2,1,0:T(2,128)(2,1)} %all-to-all-done.3) | data formatting | bytes 8388608
  586.6 0.0 copy-start.7
  586.6 0.0 copy-start.9
  586.6 9.3 %copy.46 = bf16[2,32,16,32,64]{4,3,2,1,0:T(8,128)(2,1)} copy(bf16[2,32,16,32,64]{4,3,0,1,2:T(8,128)(2,1)} %bitcast.90) | data formatting | bytes 8388608 | tf_op jit(solution)/shard_map/all_to_all | solution.py:81
  595.9 0.0 copy-done.7
  595.9 0.0 copy-done.9
  595.9 12.8 %fusion.12 = f32[2,32,512,64]{2,3,0,1:T(8,128)S(1)} fusion(f32[512]{0:T(512)S(1)} %copy-done.9, bf16[32,512,512]{2,1,0:T(8,128)(2,1)} %param.8, pred[32,512]{1,0:T(8,128)(4,1)S(1)} %copy-done.7, bf16[2,32,512,64]{3,2,1,0:T(8,128)(2,1)} %bitcast.92), kind=kOutput, calls=%fused_computation.22 | convolution fusion | flops 2181038080 | bytes 29378560 | tf_op jit(solution)/shard_map/mnl,rmlf->rmnf/dot_general | solution.py:83
  608.7 4.5 copy.50
  (1 shorter events, 0.0 us)
Async XLA Ops:
  7.2 239.0 %copy-start = (bf16[256,256]{1,0:T(8,128)(2,1)S(1)}, bf16[256,256]{1,0:T(8,128)(2,1)}, u32[]{:S(2)}) copy-start(bf16[256,256]{1,0:T(8,128)(2,1)} %param.11) | copy-start | bytes 393220
  7.3 0.6 copy-start.6
  50.6 85.1 %all-to-all-start = ((bf16[16,2,65536]{2,1,0:T(2,128)(2,1)}), bf16[16,2,65536]{2,1,0:T(2,128)(2,1)}, u32[]{:S(2)}, u32[]{:S(2)}) async-start(bf16[16,2,65536]{2,1,0:T(2,128)(2,1)} %reshape.54), calls=%async_computation | async-start | bytes 8388608 | tf_op jit(solution)/shard_map/all_to_all | solution.py:51
  186.1 51.8 %copy-start.8 = (bf16[128,256]{1,0:T(8,128)(2,1)S(1)}, bf16[128,256]{1,0:T(8,128)(2,1)}, u32[]{:S(2)}) copy-start(bf16[128,256]{1,0:T(8,128)(2,1)} %param.10) | copy-start | bytes 196612
  238.0 8.1 %copy-start.4 = (bf16[2,16,64,1024]{3,2,0,1:T(8,128)(2,1)}, bf16[2,16,64,1024]{3,2,0,1:T(8,128)(2,1)S(1)}, u32[]{:S(2)}) copy-start(bf16[2,16,64,1024]{3,2,0,1:T(8,128)(2,1)S(1)} %copy.39) | copy-start | bytes 12582916
  246.1 8.2 %copy-start.2 = (bf16[16,1024,256]{2,1,0:T(8,128)(2,1)}, bf16[16,1024,256]{2,1,0:T(8,128)(2,1)S(1)}, u32[]{:S(2)}) copy-start(bf16[16,1024,256]{2,1,0:T(8,128)(2,1)S(1)} %get-tuple-element.19) | copy-start | bytes 25165828
  246.1 11.6 %copy-start.5 = (bf16[256,128]{1,0:T(8,128)(2,1)S(1)}, bf16[256,128]{1,0:T(8,128)(2,1)}, u32[]{:S(2)}) copy-start(bf16[256,128]{1,0:T(8,128)(2,1)} %param.12) | copy-start | bytes 196612
  254.3 3.4 copy-start.1
  269.0 53.5 %all-to-all-start.2 = ((bf16[16,1024,128]{1,0,2:T(8,128)(2,1)}), bf16[16,1024,128]{1,0,2:T(8,128)(2,1)}, u32[]{:S(2)}, u32[]{:S(2)}) async-start(bf16[16,1024,128]{1,0,2:T(8,128)(2,1)} %copy.41), calls=%async_computation.2 | async-start | bytes 8388608 | tf_op jit(solution)/shard_map/all_to_all | solution.py:79
  359.9 213.1 %all-to-all-start.3 = ((bf16[16,2,65536]{2,1,0:T(2,128)(2,1)}), bf16[16,2,65536]{2,1,0:T(2,128)(2,1)}, u32[]{:S(2)}, u32[]{:S(2)}) async-start(bf16[16,2,65536]{2,1,0:T(2,128)(2,1)} %reshape.56), calls=%async_computation.3 | async-start | bytes 8388608 | tf_op jit(solution)/shard_map/all_to_all | solution.py:81
  378.7 189.5 %all-reduce.3.cloned.1.call-start = ((), (), s32[]{:S(2)}) async-start(), calls=%async_computation.4 | async-start | bytes 1048576 | tf_op jit(solution)/shard_map/psum | solution.py:73
  390.6 9.5 %copy-start.3 = (bf16[16,1024,256]{2,1,0:T(8,128)(2,1)}, bf16[16,1024,256]{2,1,0:T(8,128)(2,1)S(1)}, u32[]{:S(2)}) copy-start(bf16[16,1024,256]{2,1,0:T(8,128)(2,1)S(1)} %multiply_convert_fusion.2) | copy-start | bytes 25165828
  586.6 9.3 %copy-start.7 = (pred[32,512]{1,0:T(8,128)(4,1)S(1)}, pred[32,512]{1,0:T(8,128)(4,1)}, u32[]{:S(2)}) copy-start(pred[32,512]{1,0:T(8,128)(4,1)} %copy-done.6) | copy-start | bytes 49156
  586.6 9.3 %copy-start.9 = (f32[512]{0:T(512)S(1)}, f32[512]{0:T(512)}, u32[]{:S(2)}) copy-start(f32[512]{0:T(512)} %param.9) | copy-start | bytes 6148
Sparse Core Ops, SparseCore 0:
  414.1 154.0 all-reduce.2
where the time goes:
time: 631 us; the launch traced here: 620 us
  waiting for transfers between devices  263 us (42%)
  local copies, waits for them, and re-layouts  138 us (22%)
  matrix products  108 us (17%)
  blocking collectives  51.4 us (8%)
  starting transfers between devices  32.2 us (5%)
  between operations  14.5 us (2%)
  other arithmetic  13.6 us (2%)
    psum x1, waiting for transfers between devices, shards(): lax.psum((part_first, part_second, part_third), ('lat', 'lev'))  154 us
    all_to_all x1, waiting for transfers between devices, shards(): lax.all_to_all(fourier, 'lat', split_axis=2, concat_axis=1, tiled=True)  68.9 us
    unnamed x25, local copies, waits for them, and re-layouts  63.7 us
    all_to_all x1, blocking collectives, shards(): lax.all_to_all(grid_part, 'lev', split_axis=0, concat_axis=1, tiled=True)  51.4 us
    all_to_all x1, waiting for transfers between devices, shards(): lax.all_to_all(tend, 'lev', split_axis=2, concat_axis=0, tiled=True)  40.1 us
    all_to_all x2, local copies, waits for them, and re-layouts, shards(): lax.all_to_all(fourier, 'lat', split_axis=2, concat_axis=1, tiled=True)  21.3 us
    all_to_all x1, starting transfers between devices, shards(): lax.all_to_all(back_part, 'lat', split_axis=1, concat_axis=2, tiled=True)  18.8 us
    convert_element_type x1, local copies, waits for them, and re-layouts, shards(): fourier = jnp.einsum('mnl,rmnf->rmlf', masked, spectral, preferred_elemen...  18.6 us
  transfers between devices with their start and end apart: 4, of which 3 were waited for; matrix products, arithmetic and copies ran while one was open for 9% of the time, Pallas kernels for 0%

commit v1 on v0

v1 whole, which is shorter than its diff:
```python
import functools
import math

import jax
import jax.numpy as jnp
import ml_dtypes
import numpy as np
from jax import lax
from jax.experimental import pallas as pl
from jax.experimental.pallas import tpu as pltpu
from jax.sharding import PartitionSpec as P

CHUNKS = 2
BF16 = jnp.bfloat16
F32 = jnp.float32
AXES = ("lat", "lev")


def params(mib):
    return pltpu.CompilerParams(vmem_limit_bytes=mib << 20)


def basis_table(waves, nlon):
    phase = np.arange(waves)[:, None] * np.arange(nlon)[None, :] % nlon
    angle = phase * (2.0 * math.pi / nlon)
    factor = 1.0 / math.sqrt(nlon)
    table = np.concatenate([np.cos(angle) * factor, -np.sin(angle) * factor], axis=0)
    return table.astype(np.float32).astype(ml_dtypes.bfloat16)


def to_fourier_kernel(group, first_ref, spec_ref, leg_ref, *refs):
    outs, hold = refs[:-1], refs[-1]
    block, step = pl.program_id(0), pl.program_id(1)
    steps = pl.num_programs(1)
    per_step, degrees, lats = leg_ref.shape
    feats = spec_ref.shape[2]
    for k in range(per_step):
        place = step * per_step + k
        wave = first_ref[0] + block * group + place
        coeffs = spec_ref[:, k].reshape(2 * feats, degrees)
        degree = lax.broadcasted_iota(jnp.int32, coeffs.shape, 1)
        coeffs = jnp.where(degree >= wave, coeffs.astype(F32), 0.0).astype(BF16)
        sums = jnp.dot(coeffs, leg_ref[k], preferred_element_type=F32)
        hold[pl.ds(place, lats, stride=group), :] = sums.T

    @pl.when(step == steps - 1)
    def _():
        peers, chunk_lats = outs[0].shape[0], outs[0].shape[1]
        own = chunk_lats * len(outs)

        def move(p, carry):
            for c, out in enumerate(outs):
                start = pl.multiple_of((p * own + c * chunk_lats) * group, group)
                rows = hold[pl.ds(start, chunk_lats * group), :]
                out[pl.ds(p, 1)] = rows.astype(BF16).reshape(1, chunk_lats, group, 2 * feats)
            return carry

        lax.fori_loop(0, peers, move, 0)


def to_fourier(first, spec, legendre, peers, chunks):
    _, waves, feats, degrees = spec.shape
    lats = legendre.shape[2]
    group, per_step = min(16, waves), 4
    chunk_lats = lats // peers // chunks
    shape = (peers, chunk_lats, waves, 2 * feats)
    block = (peers, chunk_lats, group, 2 * feats)
    steps = group // per_step
    return pl.pallas_call(
        functools.partial(to_fourier_kernel, group),
        grid=(waves // group, steps),
        in_specs=[
            pl.BlockSpec(memory_space=pltpu.SMEM),
            pl.BlockSpec((2, per_step, feats, degrees), lambda b, s: (0, b * steps + s, 0, 0)),
            pl.BlockSpec((per_step, degrees, lats), lambda b, s: (b * steps + s, 0, 0)),
        ],
        out_specs=[pl.BlockSpec(block, lambda b, s: (0, 0, b, 0))] * chunks,
        out_shape=[jax.ShapeDtypeStruct(shape, BF16)] * chunks,
        scratch_shapes=[pltpu.VMEM((lats * group, 2 * feats), F32)],
        compiler_params=params(48),
        cost_estimate=pl.CostEstimate(
            flops=4 * waves * feats * degrees * lats, bytes_accessed=24 << 20, transcendentals=0
        ),
    )(first, spec, legendre)


def sigmoid(value):
    return 0.5 * jnp.tanh(0.5 * value) + 0.5


def columns_kernel(
    gauss_ref, bands_ref, cot_ref, basis_ref, basis_t_ref, w1_ref, w2_ref, w3_ref,
    back_ref, g1_ref, g2_ref, g3_ref,
    coef, grid, z1, z2, d1, d2, tend,
):
    step = pl.program_id(0)
    n_lat, n_lev, lats, own_waves, width = bands_ref.shape
    waves, part = n_lat * own_waves, width // 2
    nlon, feats = cot_ref.shape[1], cot_ref.shape[2]
    for j in range(lats):
        for r in range(2):
            pieces = [
                bands_ref[:, b, j].reshape(waves, width)[:, r * part : (r + 1) * part]
                for b in range(n_lev)
            ]
            coef[r * waves : (r + 1) * waves, j * feats : (j + 1) * feats] = jnp.concatenate(
                pieces, axis=1
            )
    grid[...] = jnp.dot(basis_t_ref[...], coef[...], preferred_element_type=F32).astype(BF16)
    tile = 256
    nt = (((1,), (1,)), ((), ()))
    for j in range(lats):
        cols = slice(j * feats, (j + 1) * feats)
        for t in range(nlon // tile):
            here = slice(t * tile, (t + 1) * tile)
            rows = slice(j * nlon + t * tile, j * nlon + (t + 1) * tile)
            cot = cot_ref[j, here]
            a1 = jnp.dot(grid[here, cols], w1_ref[...], preferred_element_type=F32)
            s1 = sigmoid(a1)
            u1 = a1 * s1
            z1[rows] = u1.astype(BF16)
            a2 = jnp.dot(u1.astype(BF16), w2_ref[...], preferred_element_type=F32)
            s2 = sigmoid(a2)
            u2 = a2 * s2
            z2[rows] = u2.astype(BF16)
            tend[here, cols] = jnp.dot(
                u2.astype(BF16), w3_ref[...], preferred_element_type=F32
            ).astype(BF16)
            e2 = lax.dot_general(cot, w3_ref[...], nt, preferred_element_type=F32)
            e2 = (e2 * (s2 + u2 * (1.0 - s2))).astype(BF16)
            d2[rows] = e2
            e1 = lax.dot_general(e2, w2_ref[...], nt, preferred_element_type=F32)
            d1[rows] = (e1 * (s1 + u1 * (1.0 - s1))).astype(BF16)

    @pl.when(step == 0)
    def _():
        g1_ref[...] = jnp.zeros_like(g1_ref)
        g2_ref[...] = jnp.zeros_like(g2_ref)
        g3_ref[...] = jnp.zeros_like(g3_ref)

    tn = (((0,), (0,)), ((), ()))
    for j in range(lats):
        cols = slice(j * feats, (j + 1) * feats)
        rows = slice(j * nlon, (j + 1) * nlon)
        g1_ref[...] += lax.dot_general(grid[:, cols], d1[rows], tn, preferred_element_type=F32)
        g3_ref[...] += lax.dot_general(z2[rows], cot_ref[j], tn, preferred_element_type=F32)
    g2_ref[...] += lax.dot_general(z1[...], d2[...], tn, preferred_element_type=F32)

    coef[...] = jnp.dot(basis_ref[...], tend[...], preferred_element_type=F32).astype(BF16)
    for j in range(lats):
        weight = gauss_ref[step * lats + j]
        for b in range(n_lev):
            at = j * feats + b * part
            pieces = [coef[r * waves : (r + 1) * waves, at : at + part] for r in range(2)]
            both = jnp.concatenate(pieces, axis=1)
            both = (both.astype(F32) * weight).astype(BF16)
            back_ref[:, b, j] = both.reshape(n_lat, own_waves, width)


def columns(gauss, bands, cot, first_lat, basis, basis_t, w1, w2, w3):
    n_lat, n_lev, lats, own_waves, width = bands.shape
    nlon, feats = cot.shape[1:]
    hidden = w1.shape[1]
    per_step = min(2, lats)
    first = first_lat // per_step
    whole = pl.BlockSpec(memory_space=pltpu.VMEM)
    block = pl.BlockSpec((n_lat, n_lev, per_step, own_waves, width), lambda s: (0, 0, s, 0, 0))
    waves2 = basis.shape[0]
    n_cols = lats * nlon
    return pl.pallas_call(
        columns_kernel,
        grid=(lats // per_step,),
        in_specs=[
            pl.BlockSpec(memory_space=pltpu.SMEM),
            block,
            pl.BlockSpec((per_step, nlon, feats), lambda s: (first + s, 0, 0)),
            whole, whole, whole, whole, whole,
        ],
        out_specs=[
            block,
            pl.BlockSpec((feats, hidden), lambda s: (0, 0)),
            pl.BlockSpec((hidden, hidden), lambda s: (0, 0)),
            pl.BlockSpec((hidden, feats), lambda s: (0, 0)),
        ],
        out_shape=[
            jax.ShapeDtypeStruct(bands.shape, BF16),
            jax.ShapeDtypeStruct((feats, hidden), F32),
            jax.ShapeDtypeStruct((hidden, hidden), F32),
            jax.ShapeDtypeStruct((hidden, feats), F32),
        ],
        scratch_shapes=[
            pltpu.VMEM((waves2, per_step * feats), BF16),
            pltpu.VMEM((nlon, per_step * feats), BF16),
            pltpu.VMEM((per_step * nlon, hidden), BF16),
            pltpu.VMEM((per_step * nlon, hidden), BF16),
            pltpu.VMEM((per_step * nlon, hidden), BF16),
            pltpu.VMEM((per_step * nlon, hidden), BF16),
            pltpu.VMEM((nlon, per_step * feats), BF16),
        ],
        compiler_params=params(48),
        cost_estimate=pl.CostEstimate(
            flops=2 * n_cols * (4 * feats * hidden + 3 * hidden * hidden + 2 * waves2 * feats),
            bytes_accessed=12 << 20,
            transcendentals=2 * n_cols * hidden,
        ),
    )(gauss, bands, cot, basis, basis_t, w1, w2, w3)


def to_spectral_kernel(group, first_ref, leg_ref, *refs):
    ins, out_ref, hold = refs[:-2], refs[-2], refs[-1]
    block, step = pl.program_id(0), pl.program_id(1)
    per_step, degrees, lats = leg_ref.shape
    feats = out_ref.shape[2]

    @pl.when(step == 0)
    def _():
        peers, chunk_lats = ins[0].shape[0], ins[0].shape[1]
        own = chunk_lats * len(ins)

        def move(p, carry):
            for c, source in enumerate(ins):
                start = pl.multiple_of((p * own + c * chunk_lats) * group, group)
                rows = source[pl.ds(p, 1)].reshape(chunk_lats * group, 2 * feats)
                hold[pl.ds(start, chunk_lats * group), :] = rows.astype(F32)
            return carry

        lax.fori_loop(0, peers, move, 0)

    for k in range(per_step):
        place = step * per_step + k
        wave = first_ref[0] + block * group + place
        rows = hold[pl.ds(place, lats, stride=group), :].astype(BF16)
        sums = jnp.dot(leg_ref[k], rows, preferred_element_type=F32).T
        degree = lax.broadcasted_iota(jnp.int32, sums.shape, 1)
        sums = jnp.where(degree >= wave, sums, 0.0)
        out_ref[:, k] = sums.reshape(2, feats, degrees)


def to_spectral(first, legendre, bands):
    waves, degrees, lats = legendre.shape
    peers, chunk_lats, _, width = bands[0].shape
    feats = width // 2
    group, per_step = min(16, waves), 4
    steps = group // per_step
    block = (peers, chunk_lats, group, width)
    return pl.pallas_call(
        functools.partial(to_spectral_kernel, group),
        grid=(waves // group, steps),
        in_specs=[
            pl.BlockSpec(memory_space=pltpu.SMEM),
            pl.BlockSpec((per_step, degrees, lats), lambda b, s: (b * steps + s, 0, 0)),
        ]
        + [pl.BlockSpec(block, lambda b, s: (0, 0, b, 0))] * len(bands),
        out_specs=pl.BlockSpec(
            (2, per_step, feats, degrees), lambda b, s: (0, b * steps + s, 0, 0)
        ),
        out_shape=jax.ShapeDtypeStruct((2, waves, feats, degrees), F32),
        scratch_shapes=[pltpu.VMEM((lats * group, width), F32)],
        compiler_params=params(48),
        cost_estimate=pl.CostEstimate(
            flops=4 * waves * feats * degrees * lats, bytes_accessed=28 << 20, transcendentals=0
        ),
    )(first, legendre, *bands)


def exchange(values):
    return lax.all_to_all(values, AXES, split_axis=0, concat_axis=0, tiled=True)


def total(parts, peers):
    flat = jnp.concatenate([p.reshape(-1, 128) for p in parts], axis=0)
    rows = flat.shape[0] // peers
    mine = exchange(flat.reshape(peers, rows, 128)).sum(axis=0)
    every = exchange(jnp.broadcast_to(mine[None], (peers, rows, 128)))
    every = every.reshape(-1, 128)
    out, at = [], 0
    for p in parts:
        size = p.size // 128
        out.append(every[at : at + size].reshape(p.shape))
        at += size
    return out


def shards(n_lat, n_lev, spectral, legendre, gauss_weights, w_first, w_second, w_third, cotangent):
    peers = n_lat * n_lev
    own_waves = legendre.shape[0]
    own_lats, nlon, _ = cotangent.shape
    chunks = min(CHUNKS, own_lats)
    chunk_lats = own_lats // chunks
    first_wave = (lax.axis_index("lat") * own_waves).astype(jnp.int32).reshape(1)
    first_lat = (lax.axis_index("lat") * n_lev + lax.axis_index("lev")) * own_lats
    gauss = lax.dynamic_slice(gauss_weights, (first_lat,), (own_lats,))
    table = basis_table(own_waves * n_lat, nlon)
    basis, basis_t = jnp.asarray(table), jnp.asarray(np.ascontiguousarray(table.T))
    spec = jnp.swapaxes(spectral, 2, 3)
    sent = to_fourier(first_wave, spec, legendre, peers, chunks)
    bands = [exchange(x) for x in sent]
    returned, grads = [], []
    for c in range(chunks):
        here = bands[c].reshape((n_lat, n_lev) + bands[c].shape[1:])
        back, *part = columns(
            lax.slice_in_dim(gauss, c * chunk_lats, (c + 1) * chunk_lats),
            here, cotangent, c * chunk_lats, basis, basis_t, w_first, w_second, w_third,
        )
        returned.append(exchange(back.reshape(bands[c].shape)))
        grads.append(part)
    factor = 1.0 / math.sqrt(gauss_weights.shape[0] * nlon)
    sums = [sum(parts[1:], parts[0]) * factor for parts in zip(*grads)]
    grad_first, grad_second, grad_third = total(sums, peers)
    out = to_spectral(first_wave, legendre, returned)
    return (jnp.swapaxes(out, 2, 3), grad_first, grad_second, grad_third)


def solution(mesh):
    in_specs = (
        P(None, "lat", None, "lev"),
        P("lat", None, None),
        P(),
        P(),
        P(),
        P(),
        P(("lat", "lev"), None, None),
    )
    out_specs = (P(None, "lat", None, "lev"), P(), P(), P())
    body = functools.partial(shards, mesh.shape["lat"], mesh.shape["lev"])
    return jax.shard_map(body, mesh=mesh, in_specs=in_specs, out_specs=out_specs, check_vma=False)
```

time: 631 us -> 307 us (0.49); the launches traced: 620 us -> 306 us
  waiting for transfers between devices: 263 us -> 65.3 us
  local copies, waits for them, and re-layouts: 138 us -> 7.31 us
  matrix products: 108 us -> 0 us
  blocking collectives: 51.4 us -> 145 us
  Pallas kernels: 0 us -> 80 us
  starting transfers between devices: 32.2 us -> 7.47 us
  between operations: 14.5 us -> 0.79 us
  other arithmetic: 13.6 us -> 0.16 us
    psum x1 -> x0, waiting for transfers between devices: 154 us -> none  [shards(): lax.psum((part_first, part_second, part_third), ('lat', 'lev'))]
    dot_general x11 -> x0, matrix products: 108 us -> none  [the longest x1 15.5 us: to_grid(): jnp.einsum('rmlf,rmo->lfo', coeffs, basis, preferred_element_type=jnp.flo...]
    all_to_all x1 -> x4, blocking collectives: 51.4 us -> 145 us  [exchange(): return lax.all_to_all(values, AXES, split_axis=0, concat_axis=0, tiled=True)]
    pallas_call x0 -> x4, Pallas kernels: none -> 80 us  [the longest x2 52.5 us: columns(): pl.pallas_call(columns_kernel, grid=(lats // per_step,), in_specs=[pl.Blo...]
    unnamed x25 -> x14, local copies, waits for them, and re-layouts: 63.7 us -> 4.24 us
    all_to_all x3 -> x2, waiting for transfers between devices: 109 us -> 65.3 us  [exchange(): return lax.all_to_all(values, AXES, split_axis=0, concat_axis=0, tiled=True)]
    convert_element_type x3 -> x0, local copies, waits for them, and re-layouts: 38.3 us -> none  [the longest x1 18.6 us: shards(): fourier = jnp.einsum('mnl,rmnf->rmlf', masked, spectral, preferred_elemen...]
    all_to_all x5 -> x0, local copies, waits for them, and re-layouts: 35.5 us -> none  [the longest x2 21.3 us: shards(): lax.all_to_all(fourier, 'lat', split_axis=2, concat_axis=1, tiled=True)]
  transfers between devices with their start and end apart: 4 -> 2, of which waited for: 3 -> 2; matrix products, arithmetic and copies ran while one was open for 9% -> 1% of each run, Pallas kernels for 0% -> 9%
where the time goes in v1:
time: 307 us; the launch traced here: 306 us
  blocking collectives  145 us (47%)
  Pallas kernels  80 us (26%)
  waiting for transfers between devices  65.3 us (21%)
  starting transfers between devices  7.47 us (2%)
  local copies, waits for them, and re-layouts  7.31 us (2%)
    all_to_all x4, blocking collectives, exchange(): return lax.all_to_all(values, AXES, split_axis=0, concat_axis=0, tiled=True)  145 us
    all_to_all x2, waiting for transfers between devices, exchange(): return lax.all_to_all(values, AXES, split_axis=0, concat_axis=0, tiled=True)  65.3 us
    pallas_call x2, Pallas kernels, columns(): pl.pallas_call(columns_kernel, grid=(lats // per_step,), in_specs=[pl.Blo...  52.5 us
    pallas_call x1, Pallas kernels, to_spectral(): pl.pallas_call(functools.partial(to_spectral_kernel, group), grid=(waves...  14.9 us
    pallas_call x1, Pallas kernels, to_fourier(): pl.pallas_call(functools.partial(to_fourier_kernel, group), grid=(waves /...  12.6 us
    all_to_all x2, starting transfers between devices, exchange(): return lax.all_to_all(values, AXES, split_axis=0, concat_axis=0, tiled=True)  7.47 us
  transfers between devices with their start and end apart: 2, of which 2 were waited for; matrix products, arithmetic and copies ran while one was open for 1% of the time, Pallas kernels for 9%

profile of v1, /device:TPU:0, one launch (start us, length us, event | category | flops | bytes accessed | tf_op | source)
XLA Modules:
  0.0 306.1 jit_solution(12110061339403831458)
XLA Ops:
  0.6 12.6 %shard_map.120 = (bf16[32,8,32,128]{3,2,1,0:T(8,128)(2,1)S(1)}, bf16[32,8,32,128]{3,2,1,0:T(8,128)(2,1)S(1)}) custom-call(s32[1]{0:T(128)} %bitcast.first_ref, bf16[2,32,64,512]{3,2,1,0:T(8,128)(2,1)} %bitcast.14, bf16[32,512,512]{2,1,0:T(8,128)(2,1)} %leg_ref.3), custom_call_target="tpu_custom_call" | custom-call | flops 2147483648 | bytes 25165824 | tf_op jit(solution)/shard_map/pallas_call | solution.py:69
  13.2 0.0 copy-start.2
  13.2 55.9 %all_to_all.30 = bf16[32,8,32,128]{3,2,1,0:T(8,128)(2,1)} all-to-all(bf16[32,8,32,128]{3,2,1,0:T(8,128)(2,1)S(1)} %get-tuple-element.16), channel_id=1, replica_groups=mesh['lat'=16,'lev'=2] {'lat','lev'}, dimensions={0} | all-to-all | bytes 4194304 | tf_op jit(solution)/shard_map/all_to_all | solution.py:267
  69.2 0.0 copy-done.2
  69.2 0.0 copy-start.4
  69.2 0.0 copy-start.5
  69.2 0.0 copy-start.6
  69.2 3.7 %all-to-all-start = ((bf16[32,8,32,128]{3,2,1,0:T(8,128)(2,1)}), bf16[32,8,32,128]{3,2,1,0:T(8,128)(2,1)S(1)}, u32[]{:S(2)}, u32[]{:S(2)}) async-start(bf16[32,8,32,128]{3,2,1,0:T(8,128)(2,1)} %copy-done.2), calls=%async_computation | async-start | bytes 4194304 | tf_op jit(solution)/shard_map/all_to_all | solution.py:267
  72.9 0.8 dynamic_slice.3
  73.6 0.1 fusion.1
  73.7 0.0 copy-done.4
  73.7 0.0 copy-done.5
  73.7 0.0 copy-done.6
  73.7 0.0 copy-start.3
  73.7 1.6 copy-done.3
  75.3 26.2 %shard_map.122 = (bf16[16,2,8,32,128]{4,3,2,1,0:T(8,128)(2,1)S(1)}, f32[128,256]{1,0:T(8,128)S(1)}, f32[256,256]{1,0:T(8,128)S(1)}, f32[256,128]{1,0:T(8,128)S(1)}) custom-call(f32[8]{0:T(128)S(1)} %get-tuple-element.26.gauss_ref, bf16[16,2,8,32,128]{4,3,2,1,0:T(8,128)(2,1)S(1)} %bitcast.12, bf16[16,1024,128]{2,1,0:T(8,128)(2,1)} %cot_ref.3, ...), custom_call_target="tpu_custom_call" | custom-call | flops 9663676416 | bytes 12582912 | tf_op jit(solution)/shard_map/pallas_call | solution.py:170
  101.5 0.0 copy-start.1
  101.5 1.3 copy-done.1
  102.9 18.7 %all-to-all-done = bf16[32,8,32,128]{3,2,1,0:T(8,128)(2,1)S(1)} async-done(((bf16[32,8,32,128]{3,2,1,0:T(8,128)(2,1)}), bf16[32,8,32,128]{3,2,1,0:T(8,128)(2,1)S(1)}, u32[]{:S(2)}, u32[]{:S(2)}) %all-to-all-start) | async-done | bytes 2097184 | tf_op jit(solution)/shard_map/all_to_all | solution.py:267
  121.6 26.2 %shard_map.121 = (bf16[16,2,8,32,128]{4,3,2,1,0:T(8,128)(2,1)S(1)}, f32[128,256]{1,0:T(8,128)S(1)}, f32[256,256]{1,0:T(8,128)S(1)}, f32[256,128]{1,0:T(8,128)S(1)}) custom-call(f32[8]{0:T(128)S(1)} %get-tuple-element.27.gauss_ref, bf16[16,2,8,32,128]{4,3,2,1,0:T(8,128)(2,1)S(1)} %bitcast.9, bf16[16,1024,128]{2,1,0:T(8,128)(2,1)} %cot_ref.3, ...), custom_call_target="tpu_custom_call" | custom-call | flops 9663676416 | bytes 12582912 | tf_op jit(solution)/shard_map/pallas_call | solution.py:170
  147.8 0.0 copy-start
  147.8 1.3 copy-done
  149.3 18.5 %all_to_all.31 = f32[32,32,128]{2,1,0:T(8,128)S(1)} all-to-all(f32[32,32,128]{2,1,0:T(8,128)S(1)} %bitcast.15), channel_id=1, replica_groups=mesh['lat'=16,'lev'=2] {'lat','lev'}, dimensions={0} | all-to-all | bytes 1048576 | tf_op jit(solution)/shard_map/all_to_all | solution.py:267
  167.9 0.1 broadcast_in_dim.2
  167.9 18.4 %all_to_all.32 = f32[32,32,128]{2,1,0:T(8,128)S(1)} all-to-all(f32[32,32,128]{2,1,0:T(8,128)S(1)} %broadcast_in_dim.2), channel_id=1, replica_groups=mesh['lat'=16,'lev'=2] {'lat','lev'}, dimensions={0} | all-to-all | bytes 1048576 | tf_op jit(solution)/shard_map/all_to_all | solution.py:267
  186.3 52.3 %all_to_all.33.refs_1_ = bf16[32,8,32,128]{3,2,1,0:T(8,128)(2,1)S(1)} all-to-all(bf16[32,8,32,128]{3,2,1,0:T(8,128)(2,1)} %bitcast.11), channel_id=1, replica_groups=mesh['lat'=16,'lev'=2] {'lat','lev'}, dimensions={0} | all-to-all | bytes 4194304 | tf_op jit(solution)/shard_map/all_to_all | solution.py:267
  238.7 3.8 %all-to-all-start.1 = ((bf16[32,8,32,128]{3,2,1,0:T(8,128)(2,1)}), bf16[32,8,32,128]{3,2,1,0:T(8,128)(2,1)}, u32[]{:S(2)}, u32[]{:S(2)}) async-start(bf16[32,8,32,128]{3,2,1,0:T(8,128)(2,1)} %bitcast.10), calls=%async_computation.1 | async-start | bytes 4194304 | tf_op jit(solution)/shard_map/all_to_all | solution.py:267
  242.5 0.8 reshape.54
  243.3 0.7 fusion
  244.0 0.7 reshape.53
  244.7 46.5 %all-to-all-done.1.refs_0_ = bf16[32,8,32,128]{3,2,1,0:T(8,128)(2,1)} async-done(((bf16[32,8,32,128]{3,2,1,0:T(8,128)(2,1)}), bf16[32,8,32,128]{3,2,1,0:T(8,128)(2,1)}, u32[]{:S(2)}, u32[]{:S(2)}) %all-to-all-start.1) | async-done | bytes 2097184 | tf_op jit(solution)/shard_map/all_to_all | solution.py:267
  291.2 14.9 %shard_map.123 = f32[2,32,64,512]{3,2,1,0:T(8,128)} custom-call(s32[1]{0:T(128)} %bitcast.first_ref, bf16[32,512,512]{2,1,0:T(8,128)(2,1)} %leg_ref.3, bf16[32,8,32,128]{3,2,1,0:T(8,128)(2,1)} %all-to-all-done.1.refs_0_, bf16[32,8,32,128]{3,2,1,0:T(8,128)(2,1)S(1)} %all_to_all.33.refs_1_), custom_call_target="tpu_custom_call" | custom-call | flops 2147483648 | bytes 29360128 | tf_op jit(solution)/shard_map/pallas_call | solution.py:246
  (8 shorter events, 0.2 us)
Async XLA Ops:
  13.2 55.9 %copy-start.2 = (bf16[32,8,32,128]{3,2,1,0:T(8,128)(2,1)}, bf16[32,8,32,128]{3,2,1,0:T(8,128)(2,1)S(1)}, u32[]{:S(2)}) copy-start(bf16[32,8,32,128]{3,2,1,0:T(8,128)(2,1)S(1)} %get-tuple-element.14) | copy-start | bytes 6291460
  69.2 4.5 %copy-start.4 = (bf16[256,256]{1,0:T(8,128)(2,1)S(1)}, bf16[256,256]{1,0:T(8,128)(2,1)}, u32[]{:S(2)}) copy-start(bf16[256,256]{1,0:T(8,128)(2,1)} %w2_ref.3) | copy-start | bytes 393220
  69.2 4.5 %copy-start.5 = (bf16[128,256]{1,0:T(8,128)(2,1)S(1)}, bf16[128,256]{1,0:T(8,128)(2,1)}, u32[]{:S(2)}) copy-start(bf16[128,256]{1,0:T(8,128)(2,1)} %w1_ref.3) | copy-start | bytes 196612
  69.2 4.5 %copy-start.6 = (bf16[256,128]{1,0:T(8,128)(2,1)S(1)}, bf16[256,128]{1,0:T(8,128)(2,1)}, u32[]{:S(2)}) copy-start(bf16[256,128]{1,0:T(8,128)(2,1)} %w3_ref.3) | copy-start | bytes 196612
  69.2 52.4 %all-to-all-start = ((bf16[32,8,32,128]{3,2,1,0:T(8,128)(2,1)}), bf16[32,8,32,128]{3,2,1,0:T(8,128)(2,1)S(1)}, u32[]{:S(2)}, u32[]{:S(2)}) async-start(bf16[32,8,32,128]{3,2,1,0:T(8,128)(2,1)} %copy-done.2), calls=%async_computation | async-start | bytes 4194304 | tf_op jit(solution)/shard_map/all_to_all | solution.py:267
  73.7 1.6 copy-start.3
  101.5 1.3 copy-start.1
  147.8 1.3 copy-start
  238.7 52.5 %all-to-all-start.1 = ((bf16[32,8,32,128]{3,2,1,0:T(8,128)(2,1)}), bf16[32,8,32,128]{3,2,1,0:T(8,128)(2,1)}, u32[]{:S(2)}, u32[]{:S(2)}) async-start(bf16[32,8,32,128]{3,2,1,0:T(8,128)(2,1)} %bitcast.10), calls=%async_computation.1 | async-start | bytes 4194304 | tf_op jit(solution)/shard_map/all_to_all | solution.py:267

commit v2 on v1

--- a/solution.py
+++ b/solution.py
@@ -10,7 +10,6 @@
 from jax.experimental.pallas import tpu as pltpu
 from jax.sharding import PartitionSpec as P
 
-CHUNKS = 2
 BF16 = jnp.bfloat16
 F32 = jnp.float32
 AXES = ("lat", "lev")
@@ -28,7 +27,7 @@
     return table.astype(np.float32).astype(ml_dtypes.bfloat16)
 
 
-def to_fourier_kernel(group, first_ref, spec_ref, leg_ref, *refs):
+def to_fourier_kernel(group, place_ref, spec_ref, leg_ref, *refs):
     outs, hold = refs[:-1], refs[-1]
     block, step = pl.program_id(0), pl.program_id(1)
     steps = pl.num_programs(1)
@@ -36,7 +35,7 @@
     feats = spec_ref.shape[2]
     for k in range(per_step):
         place = step * per_step + k
-        wave = first_ref[0] + block * group + place
+        wave = place_ref[0] + block * group + place
         coeffs = spec_ref[:, k].reshape(2 * feats, degrees)
         degree = lax.broadcasted_iota(jnp.int32, coeffs.shape, 1)
         coeffs = jnp.where(degree >= wave, coeffs.astype(F32), 0.0).astype(BF16)
@@ -58,10 +57,10 @@
         lax.fori_loop(0, peers, move, 0)
 
 
-def to_fourier(first, spec, legendre, peers, chunks):
+def to_fourier(place, spec, legendre, peers, chunks):
     _, waves, feats, degrees = spec.shape
     lats = legendre.shape[2]
-    group, per_step = min(16, waves), 4
+    group = per_step = min(16, waves)
     chunk_lats = lats // peers // chunks
     shape = (peers, chunk_lats, waves, 2 * feats)
     block = (peers, chunk_lats, group, 2 * feats)
@@ -77,11 +76,11 @@
         out_specs=[pl.BlockSpec(block, lambda b, s: (0, 0, b, 0))] * chunks,
         out_shape=[jax.ShapeDtypeStruct(shape, BF16)] * chunks,
         scratch_shapes=[pltpu.VMEM((lats * group, 2 * feats), F32)],
-        compiler_params=params(48),
+        compiler_params=params(60),
         cost_estimate=pl.CostEstimate(
             flops=4 * waves * feats * degrees * lats, bytes_accessed=24 << 20, transcendentals=0
         ),
-    )(first, spec, legendre)
+    )(place, spec, legendre)
 
 
 def sigmoid(value):
@@ -89,14 +88,15 @@
 
 
 def columns_kernel(
-    gauss_ref, bands_ref, cot_ref, basis_ref, basis_t_ref, w1_ref, w2_ref, w3_ref,
-    back_ref, g1_ref, g2_ref, g3_ref,
+    gauss_ref, bands_ref, cot_ref, basis_ref, basis_t_ref, w1_ref, w2_ref, w3_ref, start_ref,
+    back_ref, sums_ref,
     coef, grid, z1, z2, d1, d2, tend,
 ):
     step = pl.program_id(0)
     n_lat, n_lev, lats, own_waves, width = bands_ref.shape
     waves, part = n_lat * own_waves, width // 2
     nlon, feats = cot_ref.shape[1], cot_ref.shape[2]
+    hidden = w2_ref.shape[0]
     for j in range(lats):
         for r in range(2):
             pieces = [
@@ -134,17 +134,20 @@
 
     @pl.when(step == 0)
     def _():
-        g1_ref[...] = jnp.zeros_like(g1_ref)
-        g2_ref[...] = jnp.zeros_like(g2_ref)
-        g3_ref[...] = jnp.zeros_like(g3_ref)
+        sums_ref[...] = start_ref[...]
 
     tn = (((0,), (0,)), ((), ()))
     for j in range(lats):
         cols = slice(j * feats, (j + 1) * feats)
         rows = slice(j * nlon, (j + 1) * nlon)
-        g1_ref[...] += lax.dot_general(grid[:, cols], d1[rows], tn, preferred_element_type=F32)
-        g3_ref[...] += lax.dot_general(z2[rows], cot_ref[j], tn, preferred_element_type=F32)
-    g2_ref[...] += lax.dot_general(z1[...], d2[...], tn, preferred_element_type=F32)
+        first = lax.dot_general(grid[:, cols], d1[rows], tn, preferred_element_type=F32)
+        third = lax.dot_general(z2[rows], cot_ref[j], tn, preferred_element_type=F32)
+        for h in range(hidden // feats):
+            sums_ref[h * feats : (h + 1) * feats] += first[:, h * feats : (h + 1) * feats]
+        sums_ref[2 * hidden + hidden :] += third
+    second = lax.dot_general(z1[...], d2[...], tn, preferred_element_type=F32)
+    for h in range(hidden // feats):
+        sums_ref[(h + 1) * hidden : (h + 2) * hidden] += second[:, h * feats : (h + 1) * feats]
 
     coef[...] = jnp.dot(basis_ref[...], tend[...], preferred_element_type=F32).astype(BF16)
     for j in range(lats):
@@ -157,16 +160,16 @@
             back_ref[:, b, j] = both.reshape(n_lat, own_waves, width)
 
 
-def columns(gauss, bands, cot, first_lat, basis, basis_t, w1, w2, w3):
+def columns(gauss, bands, cot, first_lat, basis, basis_t, w1, w2, w3, start):
     n_lat, n_lev, lats, own_waves, width = bands.shape
     nlon, feats = cot.shape[1:]
     hidden = w1.shape[1]
     per_step = min(2, lats)
     first = first_lat // per_step
-    whole = pl.BlockSpec(memory_space=pltpu.VMEM)
     block = pl.BlockSpec((n_lat, n_lev, per_step, own_waves, width), lambda s: (0, 0, s, 0, 0))
     waves2 = basis.shape[0]
     n_cols = lats * nlon
+    fixed = [basis, basis_t, w1, w2, w3, start]
     return pl.pallas_call(
         columns_kernel,
         grid=(lats // per_step,),
@@ -174,19 +177,12 @@
             pl.BlockSpec(memory_space=pltpu.SMEM),
             block,
             pl.BlockSpec((per_step, nlon, feats), lambda s: (first + s, 0, 0)),
-            whole, whole, whole, whole, whole,
-        ],
-        out_specs=[
-            block,
-            pl.BlockSpec((feats, hidden), lambda s: (0, 0)),
-            pl.BlockSpec((hidden, hidden), lambda s: (0, 0)),
-            pl.BlockSpec((hidden, feats), lambda s: (0, 0)),
-        ],
+        ]
+        + [pl.BlockSpec(a.shape, lambda s: (0, 0)) for a in fixed],
+        out_specs=[block, pl.BlockSpec(start.shape, lambda s: (0, 0))],
         out_shape=[
             jax.ShapeDtypeStruct(bands.shape, BF16),
-            jax.ShapeDtypeStruct((feats, hidden), F32),
-            jax.ShapeDtypeStruct((hidden, hidden), F32),
-            jax.ShapeDtypeStruct((hidden, feats), F32),
+            jax.ShapeDtypeStruct(start.shape, F32),
         ],
         scratch_shapes=[
             pltpu.VMEM((waves2, per_step * feats), BF16),
@@ -197,16 +193,16 @@
             pltpu.VMEM((per_step * nlon, hidden), BF16),
             pltpu.VMEM((nlon, per_step * feats), BF16),
         ],
-        compiler_params=params(48),
+        compiler_params=params(60),
         cost_estimate=pl.CostEstimate(
             flops=2 * n_cols * (4 * feats * hidden + 3 * hidden * hidden + 2 * waves2 * feats),
             bytes_accessed=12 << 20,
             transcendentals=2 * n_cols * hidden,
         ),
-    )(gauss, bands, cot, basis, basis_t, w1, w2, w3)
-
-
-def to_spectral_kernel(group, first_ref, leg_ref, *refs):
+    )(gauss, bands, cot, *fixed)
+
+
+def to_spectral_kernel(group, place_ref, leg_ref, *refs):
     ins, out_ref, hold = refs[:-2], refs[-2], refs[-1]
     block, step = pl.program_id(0), pl.program_id(1)
     per_step, degrees, lats = leg_ref.shape
@@ -228,7 +224,7 @@
 
     for k in range(per_step):
         place = step * per_step + k
-        wave = first_ref[0] + block * group + place
+        wave = place_ref[0] + block * group + place
         rows = hold[pl.ds(place, lats, stride=group), :].astype(BF16)
         sums = jnp.dot(leg_ref[k], rows, preferred_element_type=F32).T
         degree = lax.broadcasted_iota(jnp.int32, sums.shape, 1)
@@ -236,11 +232,11 @@
         out_ref[:, k] = sums.reshape(2, feats, degrees)
 
 
-def to_spectral(first, legendre, bands):
+def to_spectral(place, legendre, bands, chunk_lats):
     waves, degrees, lats = legendre.shape
-    peers, chunk_lats, _, width = bands[0].shape
+    peers, _, _, width = bands[0].shape
     feats = width // 2
-    group, per_step = min(16, waves), 4
+    group, per_step = min(16, waves), 8
     steps = group // per_step
     block = (peers, chunk_lats, group, width)
     return pl.pallas_call(
@@ -256,58 +252,78 @@
         ),
         out_shape=jax.ShapeDtypeStruct((2, waves, feats, degrees), F32),
         scratch_shapes=[pltpu.VMEM((lats * group, width), F32)],
-        compiler_params=params(48),
+        compiler_params=params(60),
         cost_estimate=pl.CostEstimate(
             flops=4 * waves * feats * degrees * lats, bytes_accessed=28 << 20, transcendentals=0
         ),
-    )(first, legendre, *bands)
+    )(place, legendre, *bands)
 
 
 def exchange(values):
     return lax.all_to_all(values, AXES, split_axis=0, concat_axis=0, tiled=True)
 
 
-def total(parts, peers):
-    flat = jnp.concatenate([p.reshape(-1, 128) for p in parts], axis=0)
-    rows = flat.shape[0] // peers
-    mine = exchange(flat.reshape(peers, rows, 128)).sum(axis=0)
-    every = exchange(jnp.broadcast_to(mine[None], (peers, rows, 128)))
-    every = every.reshape(-1, 128)
-    out, at = [], 0
-    for p in parts:
-        size = p.size // 128
-        out.append(every[at : at + size].reshape(p.shape))
-        at += size
-    return out
+def sum_over_lev(values, n_lev):
+    me = lax.axis_index("lev")
+    half = n_lev // 2
+    while half:
+        upper = jnp.where(me & half != 0, half, 0)
+        kept = lax.dynamic_slice_in_dim(values, upper, half, axis=0)
+        sent = lax.dynamic_slice_in_dim(values, half - upper, half, axis=0)
+        values = kept + lax.ppermute(sent, "lev", [(i, i ^ half) for i in range(n_lev)])
+        half //= 2
+    return values[0]
+
+
+def split_values(values):
+    high = values.astype(BF16)
+    return jnp.stack([high, (values - high.astype(F32)).astype(BF16)], axis=1)
 
 
 def shards(n_lat, n_lev, spectral, legendre, gauss_weights, w_first, w_second, w_third, cotangent):
     peers = n_lat * n_lev
     own_waves = legendre.shape[0]
-    own_lats, nlon, _ = cotangent.shape
-    chunks = min(CHUNKS, own_lats)
-    chunk_lats = own_lats // chunks
-    first_wave = (lax.axis_index("lat") * own_waves).astype(jnp.int32).reshape(1)
-    first_lat = (lax.axis_index("lat") * n_lev + lax.axis_index("lev")) * own_lats
-    gauss = lax.dynamic_slice(gauss_weights, (first_lat,), (own_lats,))
+    own_lats, nlon, feats = cotangent.shape
+    hidden = w_first.shape[1]
+    width = 2 * spectral.shape[3]
+    lats = own_lats // 2
+    lat, lev = lax.axis_index("lat"), lax.axis_index("lev")
+    place = (lat * own_waves).astype(jnp.int32).reshape(1)
+    gauss = lax.dynamic_slice(gauss_weights, ((lat * n_lev + lev) * own_lats,), (own_lats,))
     table = basis_table(own_waves * n_lat, nlon)
     basis, basis_t = jnp.asarray(table), jnp.asarray(np.ascontiguousarray(table.T))
+    tables = (basis, basis_t, w_first, w_second, w_third)
     spec = jnp.swapaxes(spectral, 2, 3)
-    sent = to_fourier(first_wave, spec, legendre, peers, chunks)
-    bands = [exchange(x) for x in sent]
-    returned, grads = [], []
-    for c in range(chunks):
-        here = bands[c].reshape((n_lat, n_lev) + bands[c].shape[1:])
-        back, *part = columns(
-            lax.slice_in_dim(gauss, c * chunk_lats, (c + 1) * chunk_lats),
-            here, cotangent, c * chunk_lats, basis, basis_t, w_first, w_second, w_third,
-        )
-        returned.append(exchange(back.reshape(bands[c].shape)))
-        grads.append(part)
-    factor = 1.0 / math.sqrt(gauss_weights.shape[0] * nlon)
-    sums = [sum(parts[1:], parts[0]) * factor for parts in zip(*grads)]
-    grad_first, grad_second, grad_third = total(sums, peers)
-    out = to_spectral(first_wave, legendre, returned)
+    n_sums = 2 * feats * hidden + hidden * hidden
+
+    shape = (n_lat, n_lev, lats, own_waves, width)
+    one, two = [exchange(x) for x in to_fourier(place, spec, legendre, peers, 2)]
+    sums = jnp.zeros((n_sums // feats, feats), F32)
+    back_one, sums = columns(gauss[:lats], one.reshape(shape), cotangent, 0, *tables, sums)
+    back_one = exchange(back_one.reshape(one.shape))
+    back_two, sums = columns(gauss[lats:], two.reshape(shape), cotangent, lats, *tables, sums)
+
+    sums = sum_over_lev(sums.reshape(n_lev, -1, feats), n_lev).reshape(peers, -1)
+    size = sums.shape[1]
+    pairs = split_values(sums).reshape(peers, -1)
+    unit = own_waves * width
+    pairs = jnp.pad(pairs, ((0, 0), (0, -pairs.shape[1] % unit)))
+    pairs = pairs.reshape(peers, -1, own_waves, width)
+    back_two = jnp.concatenate([back_two.reshape(two.shape), pairs], axis=1)
+    back_one, back_two = lax.optimization_barrier((back_one, back_two))
+    back_two = exchange(back_two)
+    pairs = back_two[:, lats:].reshape(n_lat, n_lev, -1)[:, :, : 2 * size]
+    pairs = pairs.reshape(n_lat, n_lev, 2, size).astype(F32)
+    share = pairs.sum(axis=(0, 2)) * (1.0 / math.sqrt(gauss_weights.shape[0] * nlon))
+    every = exchange(jnp.broadcast_to(share[None], (peers, n_lev, size)))
+    every = jnp.swapaxes(every, 0, 1).reshape(-1, feats)
+
+    out = to_spectral(place, legendre, [back_one, back_two], lats)
+    halves = hidden // feats
+    first, second = every[: halves * feats], every[halves * feats : halves * (feats + hidden)]
+    grad_first = jnp.concatenate(jnp.split(first, halves), axis=1)
+    grad_second = jnp.concatenate(jnp.split(second, halves), axis=1)
+    grad_third = every[halves * (feats + hidden) :]
     return (jnp.swapaxes(out, 2, 3), grad_first, grad_second, grad_third)
 
 

time: 307 us -> 255 us (0.83)
  blocking collectives: 145 us -> 114 us
  waiting for transfers between devices: 65.3 us -> 35.1 us
  starting transfers between devices: 7.47 us -> 12.6 us
  other arithmetic: 0.16 us -> 5.22 us
    all_to_all x2 -> x3, waiting for transfers between devices: 65.3 us -> 27 us  [exchange(): return lax.all_to_all(values, AXES, split_axis=0, concat_axis=0, tiled=True)]
    all_to_all x4 -> x2, blocking collectives: 145 us -> 114 us  [exchange(): return lax.all_to_all(values, AXES, split_axis=0, concat_axis=0, tiled=True)]
    ppermute x0 -> x1, waiting for transfers between devices: none -> 8.11 us  [sum_over_lev(): lax.ppermute(sent, 'lev', [(i, i ^ half) for i in range(n_lev)])]
    unnamed x14 -> x6, local copies, waits for them, and re-layouts: 4.24 us -> 0.01 us
    all_to_all x2 -> x3, starting transfers between devices: 7.47 us -> 11 us  [exchange(): return lax.all_to_all(values, AXES, split_axis=0, concat_axis=0, tiled=True)]
  transfers between devices with their start and end apart: 2 -> 4, of which waited for: 2 -> 4; matrix products, arithmetic and copies ran while one was open for 1% -> 3% of each run, Pallas kernels for 9% -> 27%
where the time goes in v2:
time: 255 us; the launch traced here: 254 us
  blocking collectives  114 us (45%)
  Pallas kernels  80 us (31%)
  waiting for transfers between devices  35.1 us (14%)
  starting transfers between devices  12.6 us (5%)
  local copies, waits for them, and re-layouts  5.88 us (2%)
  other arithmetic  5.22 us (2%)
    all_to_all x2, blocking collectives, exchange(): return lax.all_to_all(values, AXES, split_axis=0, concat_axis=0, tiled=True)  114 us
    pallas_call x2, Pallas kernels, columns(): pl.pallas_call(columns_kernel, grid=(lats // per_step,), in_specs=[pl.Blo...  54.8 us
    all_to_all x3, waiting for transfers between devices, exchange(): return lax.all_to_all(values, AXES, split_axis=0, concat_axis=0, tiled=True)  27 us
    pallas_call x1, Pallas kernels, to_spectral(): pl.pallas_call(functools.partial(to_spectral_kernel, group), grid=(waves...  13.6 us
    pallas_call x1, Pallas kernels, to_fourier(): pl.pallas_call(functools.partial(to_fourier_kernel, group), grid=(waves /...  11.5 us
    all_to_all x3, starting transfers between devices, exchange(): return lax.all_to_all(values, AXES, split_axis=0, concat_axis=0, tiled=True)  11 us
    ppermute x1, waiting for transfers between devices, sum_over_lev(): lax.ppermute(sent, 'lev', [(i, i ^ half) for i in range(n_lev)])  8.11 us
  transfers between devices with their start and end apart: 4, of which 4 were waited for; matrix products, arithmetic and copies ran while one was open for 3% of the time, Pallas kernels for 27%

profile of v2, /device:TPU:0, one launch (start us, length us, event | category | flops | bytes accessed | tf_op | source)
XLA Modules:
  0.0 254.0 jit_solution(14605142868107295446)
XLA Ops:
  0.6 11.5 %shard_map.120 = (bf16[32,8,32,128]{3,2,1,0:T(8,128)(2,1)}, bf16[32,8,32,128]{3,2,1,0:T(8,128)(2,1)}) custom-call(s32[1]{0:T(128)} %bitcast.place_ref, bf16[2,32,64,512]{3,2,1,0:T(8,128)(2,1)} %bitcast.13, bf16[32,512,512]{2,1,0:T(8,128)(2,1)} %leg_ref.3), custom_call_target="tpu_custom_call" | custom-call | flops 2147483648 | bytes 25165824 | tf_op jit(solution)/shard_map/pallas_call | solution.py:68
  12.2 56.1 %all_to_all.25 = bf16[32,8,32,128]{3,2,1,0:T(8,128)(2,1)} all-to-all(bf16[32,8,32,128]{3,2,1,0:T(8,128)(2,1)} %get-tuple-element.12), channel_id=1, replica_groups=mesh['lat'=16,'lev'=2] {'lat','lev'}, dimensions={0} | all-to-all | bytes 4194304 | tf_op jit(solution)/shard_map/all_to_all | solution.py:263
  68.3 3.7 %all-to-all-start.2 = ((bf16[32,8,32,128]{3,2,1,0:T(8,128)(2,1)}), bf16[32,8,32,128]{3,2,1,0:T(8,128)(2,1)S(1)}, u32[]{:S(2)}, u32[]{:S(2)}) async-start(bf16[32,8,32,128]{3,2,1,0:T(8,128)(2,1)} %get-tuple-element.14), calls=%async_computation.2 | async-start | bytes 4194304 | tf_op jit(solution)/shard_map/all_to_all | solution.py:263
  72.0 0.8 dynamic_slice.9
  72.7 0.6 fusion.2
  73.3 0.8 broadcast_in_dim.4.start_ref
  74.1 27.4 %shard_map.121 = (bf16[16,2,8,32,128]{4,3,2,1,0:T(8,128)(2,1)}, f32[1024,128]{1,0:T(8,128)}) custom-call(f32[8]{0:T(128)} %get-tuple-element.26.gauss_ref, bf16[16,2,8,32,128]{4,3,2,1,0:T(8,128)(2,1)} %bitcast.18, bf16[16,1024,128]{2,1,0:T(8,128)(2,1)} %cot_ref.3, bf16[1024,1024]{1,0:T(8,128)(2,1)} %constant.32.clone.basis_ref, ...), custom_call_target="tpu_custom_call" | custom-call | flops 9663676416 | bytes 12582912 | tf_op jit(solution)/shard_map/pallas_call | solution.py:173
  101.5 19.2 %all-to-all-done.2 = bf16[32,8,32,128]{3,2,1,0:T(8,128)(2,1)S(1)} async-done(((bf16[32,8,32,128]{3,2,1,0:T(8,128)(2,1)}), bf16[32,8,32,128]{3,2,1,0:T(8,128)(2,1)S(1)}, u32[]{:S(2)}, u32[]{:S(2)}) %all-to-all-start.2) | async-done | bytes 2097184 | tf_op jit(solution)/shard_map/all_to_all | solution.py:263
  120.7 0.0 copy-start.1
  120.7 4.0 %all-to-all-start.1 = ((bf16[32,8,32,128]{3,2,1,0:T(8,128)(2,1)}), bf16[32,8,32,128]{3,2,1,0:T(8,128)(2,1)}, u32[]{:S(2)}, u32[]{:S(2)}) async-start(bf16[32,8,32,128]{3,2,1,0:T(8,128)(2,1)} %bitcast.17), calls=%async_computation.1 | async-start | bytes 4194304 | tf_op jit(solution)/shard_map/all_to_all | solution.py:263
  124.7 0.0 copy-done.1
  124.7 27.5 %shard_map.122 = (bf16[16,2,8,32,128]{4,3,2,1,0:T(8,128)(2,1)}, f32[1024,128]{1,0:T(8,128)}) custom-call(f32[8]{0:T(128)} %get-tuple-element.25.gauss_ref, bf16[16,2,8,32,128]{4,3,2,1,0:T(8,128)(2,1)} %bitcast.16, bf16[16,1024,128]{2,1,0:T(8,128)(2,1)} %cot_ref.3, bf16[1024,1024]{1,0:T(8,128)(2,1)} %constant.32.clone.basis_ref, ...), custom_call_target="tpu_custom_call" | custom-call | flops 9663676416 | bytes 12582912 | tf_op jit(solution)/shard_map/pallas_call | solution.py:173
  152.2 0.0 copy-start.2
  152.2 1.1 constant_dynamic-slice_fusion
  153.3 1.6 collective-permute-start
  154.9 8.1 %collective-permute-done = f32[1,512,128]{2,1,0:T(8,128)S(1)} collective-permute-done((f32[1,512,128]{2,1,0:T(8,128)S(1)}, f32[1,512,128]{2,1,0:T(8,128)S(1)}, u32[]{:S(2)}, u32[]{:S(2)}) %collective-permute-start) | collective-permute-done | bytes 262176 | tf_op jit(solution)/shard_map/ppermute | solution.py:273
  163.0 1.0 dynamic-slice_add_fusion
  164.0 0.2 convert_element_type.44
  164.2 0.2 subtract_convert_fusion
  164.4 0.6 pad_maximum_fusion.1
  165.0 0.2 reshape.74
  165.2 0.0 copy-done.2
  165.2 1.6 pad_maximum_fusion
  166.8 6.4 %all-to-all-done.1.refs_0_ = bf16[32,8,32,128]{3,2,1,0:T(8,128)(2,1)} async-done(((bf16[32,8,32,128]{3,2,1,0:T(8,128)(2,1)}), bf16[32,8,32,128]{3,2,1,0:T(8,128)(2,1)}, u32[]{:S(2)}, u32[]{:S(2)}) %all-to-all-start.1) | async-done | bytes 2097184 | tf_op jit(solution)/shard_map/all_to_all | solution.py:263
  173.2 58.3 %all_to_all.26.refs_1_ = bf16[32,9,32,128]{3,2,1,0:T(8,128)(2,1)S(1)} all-to-all(bf16[32,9,32,128]{3,2,1,0:T(8,128)(2,1)} %pad_maximum_fusion), channel_id=1, replica_groups=mesh['lat'=16,'lev'=2] {'lat','lev'}, dimensions={0} | all-to-all | bytes 4718592 | tf_op jit(solution)/shard_map/all_to_all | solution.py:263
  231.5 0.0 copy-start
  231.5 0.1 slice_convert_fusion
  231.6 0.3 reshape.76
  231.9 0.2 reduce_sum.9
  232.1 1.0 broadcast_in_dim.10
  233.2 3.3 %all-to-all-start.4 = ((f32[32,2,2048]{2,1,0:T(2,128)}), f32[32,2,2048]{2,1,0:T(2,128)S(1)}, u32[]{:S(2)}, u32[]{:S(2)}) async-start(f32[32,2,2048]{2,1,0:T(2,128)} %broadcast_in_dim.10), calls=%async_computation.4 | async-start | bytes 1048576 | tf_op jit(solution)/shard_map/all_to_all | solution.py:263
  236.5 0.0 copy-done
  236.5 13.6 %shard_map.123 = f32[2,32,64,512]{3,2,1,0:T(8,128)} custom-call(s32[1]{0:T(128)} %bitcast.place_ref, bf16[32,512,512]{2,1,0:T(8,128)(2,1)} %leg_ref.3, bf16[32,8,32,128]{3,2,1,0:T(8,128)(2,1)} %all-to-all-done.1.refs_0_, bf16[32,9,32,128]{3,2,1,0:T(8,128)(2,1)} %copy-done), custom_call_target="tpu_custom_call" | custom-call | flops 2147483648 | bytes 29360128 | tf_op jit(solution)/shard_map/pallas_call | solution.py:242
  250.1 1.4 all-to-all-done.4
  251.5 0.3 copy.13
  251.8 0.1 reshape.75
  251.9 0.7 fusion
  252.6 0.7 pad_maximum_fusion.3
  253.3 0.7 pad_maximum_fusion.2
  (2 shorter events, 0.0 us)
Async XLA Ops:
  68.3 52.4 %all-to-all-start.2 = ((bf16[32,8,32,128]{3,2,1,0:T(8,128)(2,1)}), bf16[32,8,32,128]{3,2,1,0:T(8,128)(2,1)S(1)}, u32[]{:S(2)}, u32[]{:S(2)}) async-start(bf16[32,8,32,128]{3,2,1,0:T(8,128)(2,1)} %get-tuple-element.14), calls=%async_computation.2 | async-start | bytes 4194304 | tf_op jit(solution)/shard_map/all_to_all | solution.py:263
  120.7 4.0 %copy-start.1 = (bf16[32,8,32,128]{3,2,1,0:T(8,128)(2,1)}, bf16[32,8,32,128]{3,2,1,0:T(8,128)(2,1)S(1)}, u32[]{:S(2)}) copy-start(bf16[32,8,32,128]{3,2,1,0:T(8,128)(2,1)S(1)} %all-to-all-done.2) | copy-start | bytes 6291460
  120.7 52.5 %all-to-all-start.1 = ((bf16[32,8,32,128]{3,2,1,0:T(8,128)(2,1)}), bf16[32,8,32,128]{3,2,1,0:T(8,128)(2,1)}, u32[]{:S(2)}, u32[]{:S(2)}) async-start(bf16[32,8,32,128]{3,2,1,0:T(8,128)(2,1)} %bitcast.17), calls=%async_computation.1 | async-start | bytes 4194304 | tf_op jit(solution)/shard_map/all_to_all | solution.py:263
  152.2 13.0 %copy-start.2 = (bf16[16,2,8,32,128]{4,3,2,1,0:T(8,128)(2,1)S(1)}, bf16[16,2,8,32,128]{4,3,2,1,0:T(8,128)(2,1)}, u32[]{:S(2)}) copy-start(bf16[16,2,8,32,128]{4,3,2,1,0:T(8,128)(2,1)} %get-tuple-element.16) | copy-start | bytes 6291460
  153.3 9.7 %collective-permute-start = (f32[1,512,128]{2,1,0:T(8,128)S(1)}, f32[1,512,128]{2,1,0:T(8,128)S(1)}, u32[]{:S(2)}, u32[]{:S(2)}) collective-permute-start(f32[1,512,128]{2,1,0:T(8,128)S(1)} %constant_dynamic-slice_fusion), channel_id=1, source_target_pairs={{0,1},{1,0},{2,3},{3,2},{4,5},{5,4},{6,7},{7,6},{8,9},{9,8},{10,11... | collective-permute-start | bytes 786440 | tf_op jit(solution)/shard_map/ppermute | solution.py:273
  231.5 5.0 %copy-start = (bf16[32,9,32,128]{3,2,1,0:T(8,128)(2,1)}, bf16[32,9,32,128]{3,2,1,0:T(8,128)(2,1)S(1)}, u32[]{:S(2)}) copy-start(bf16[32,9,32,128]{3,2,1,0:T(8,128)(2,1)S(1)} %all_to_all.26.refs_1_) | copy-start | bytes 7077892
  233.2 18.4 %all-to-all-start.4 = ((f32[32,2,2048]{2,1,0:T(2,128)}), f32[32,2,2048]{2,1,0:T(2,128)S(1)}, u32[]{:S(2)}, u32[]{:S(2)}) async-start(f32[32,2,2048]{2,1,0:T(2,128)} %broadcast_in_dim.10), calls=%async_computation.4 | async-start | bytes 1048576 | tf_op jit(solution)/shard_map/all_to_all | solution.py:263

commit v3 on v2

--- a/solution.py
+++ b/solution.py
@@ -19,6 +19,10 @@
     return pltpu.CompilerParams(vmem_limit_bytes=mib << 20)
 
 
+def in_hbm(values):
+    return pltpu.with_memory_space_constraint(values, pltpu.HBM)
+
+
 def basis_table(waves, nlon):
     phase = np.arange(waves)[:, None] * np.arange(nlon)[None, :] % nlon
     angle = phase * (2.0 * math.pi / nlon)
@@ -27,55 +31,88 @@
     return table.astype(np.float32).astype(ml_dtypes.bfloat16)
 
 
-def to_fourier_kernel(group, place_ref, spec_ref, leg_ref, *refs):
-    outs, hold = refs[:-1], refs[-1]
-    block, step = pl.program_id(0), pl.program_id(1)
-    steps = pl.num_programs(1)
-    per_step, degrees, lats = leg_ref.shape
+def to_fourier_kernel(group, per_step, place_ref, spec_ref, leg_ref, *refs):
+    chunks = (len(refs) - 6) // 2
+    outs, stages = refs[:chunks], refs[chunks : 2 * chunks]
+    spec, leg, hold, spec_sem, leg_sem, out_sem = refs[2 * chunks :]
+    waves, degrees, lats = leg_ref.shape
     feats = spec_ref.shape[2]
-    for k in range(per_step):
-        place = step * per_step + k
-        wave = place_ref[0] + block * group + place
-        coeffs = spec_ref[:, k].reshape(2 * feats, degrees)
-        degree = lax.broadcasted_iota(jnp.int32, coeffs.shape, 1)
-        coeffs = jnp.where(degree >= wave, coeffs.astype(F32), 0.0).astype(BF16)
-        sums = jnp.dot(coeffs, leg_ref[k], preferred_element_type=F32)
-        hold[pl.ds(place, lats, stride=group), :] = sums.T
-
-    @pl.when(step == steps - 1)
-    def _():
-        peers, chunk_lats = outs[0].shape[0], outs[0].shape[1]
-        own = chunk_lats * len(outs)
+    peers, chunk_lats = outs[0].shape[:2]
+    own = chunk_lats * chunks
+
+    def copies(step):
+        here = pl.ds(step * per_step, per_step)
+        return [
+            pltpu.make_async_copy(leg_ref.at[here], leg.at[here], leg_sem.at[step]),
+            pltpu.make_async_copy(spec_ref.at[:, here], spec.at[:, here], spec_sem.at[step]),
+        ]
+
+    def start(step, carry):
+        for copy in copies(step):
+            copy.start()
+        return carry
+
+    lax.fori_loop(0, waves // per_step, start, 0)
+    sends = []
+    for block in range(waves // group):
+
+        def work(step, carry):
+            for copy in copies(block * (group // per_step) + step):
+                copy.wait()
+            for k in range(per_step):
+                place = step * per_step + k
+                own_wave = block * group + place
+                coeffs = spec[:, own_wave].reshape(2 * feats, degrees)
+                degree = lax.broadcasted_iota(jnp.int32, coeffs.shape, 1)
+                keep = degree >= place_ref[0] + own_wave
+                coeffs = jnp.where(keep, coeffs.astype(F32), 0.0).astype(BF16)
+                sums = jnp.dot(coeffs, leg[own_wave], preferred_element_type=F32)
+                hold[pl.ds(place, lats, stride=group), :] = sums.T
+            return carry
+
+        lax.fori_loop(0, group // per_step, work, 0)
 
         def move(p, carry):
-            for c, out in enumerate(outs):
-                start = pl.multiple_of((p * own + c * chunk_lats) * group, group)
-                rows = hold[pl.ds(start, chunk_lats * group), :]
-                out[pl.ds(p, 1)] = rows.astype(BF16).reshape(1, chunk_lats, group, 2 * feats)
+            for c in range(chunks):
+                first = pl.multiple_of((p * own + c * chunk_lats) * group, group)
+                rows = hold[pl.ds(first, chunk_lats * group), :].astype(BF16)
+                rows = rows.reshape(1, 1, chunk_lats, group, 2 * feats)
+                stages[c][block : block + 1, pl.ds(p, 1)] = rows
             return carry
 
         lax.fori_loop(0, peers, move, 0)
+        for c in range(chunks):
+            there = outs[c].at[:, :, block * group : (block + 1) * group]
+            sends.append(
+                pltpu.make_async_copy(stages[c].at[block], there, out_sem.at[block, c])
+            )
+            sends[-1].start()
+    for send in sends:
+        send.wait()
 
 
 def to_fourier(place, spec, legendre, peers, chunks):
     _, waves, feats, degrees = spec.shape
     lats = legendre.shape[2]
-    group = per_step = min(16, waves)
+    group = min(16, waves)
+    per_step = min(4, group)
     chunk_lats = lats // peers // chunks
     shape = (peers, chunk_lats, waves, 2 * feats)
-    block = (peers, chunk_lats, group, 2 * feats)
-    steps = group // per_step
+    stage = (waves // group, peers, chunk_lats, group, 2 * feats)
     return pl.pallas_call(
-        functools.partial(to_fourier_kernel, group),
-        grid=(waves // group, steps),
-        in_specs=[
-            pl.BlockSpec(memory_space=pltpu.SMEM),
-            pl.BlockSpec((2, per_step, feats, degrees), lambda b, s: (0, b * steps + s, 0, 0)),
-            pl.BlockSpec((per_step, degrees, lats), lambda b, s: (b * steps + s, 0, 0)),
+        functools.partial(to_fourier_kernel, group, per_step),
+        in_specs=[pl.BlockSpec(memory_space=pltpu.SMEM)] + [pl.BlockSpec(memory_space=pl.ANY)] * 2,
+        out_specs=[pl.BlockSpec(memory_space=pl.ANY)] * chunks,
+        out_shape=[jax.ShapeDtypeStruct(shape, BF16)] * chunks,
+        scratch_shapes=[pltpu.VMEM(stage, BF16)] * chunks
+        + [
+            pltpu.VMEM(spec.shape, BF16),
+            pltpu.VMEM(legendre.shape, BF16),
+            pltpu.VMEM((lats * group, 2 * feats), F32),
+            pltpu.SemaphoreType.DMA((waves // per_step,)),
+            pltpu.SemaphoreType.DMA((waves // per_step,)),
+            pltpu.SemaphoreType.DMA((waves // group, chunks)),
         ],
-        out_specs=[pl.BlockSpec(block, lambda b, s: (0, 0, b, 0))] * chunks,
-        out_shape=[jax.ShapeDtypeStruct(shape, BF16)] * chunks,
-        scratch_shapes=[pltpu.VMEM((lats * group, 2 * feats), F32)],
         compiler_params=params(60),
         cost_estimate=pl.CostEstimate(
             flops=4 * waves * feats * degrees * lats, bytes_accessed=24 << 20, transcendentals=0
@@ -181,7 +218,7 @@
         + [pl.BlockSpec(a.shape, lambda s: (0, 0)) for a in fixed],
         out_specs=[block, pl.BlockSpec(start.shape, lambda s: (0, 0))],
         out_shape=[
-            jax.ShapeDtypeStruct(bands.shape, BF16),
+            pltpu.HBM(bands.shape, BF16),
             jax.ShapeDtypeStruct(start.shape, F32),
         ],
         scratch_shapes=[
@@ -193,84 +230,147 @@
             pltpu.VMEM((per_step * nlon, hidden), BF16),
             pltpu.VMEM((nlon, per_step * feats), BF16),
         ],
-        compiler_params=params(60),
+        compiler_params=params(44),
         cost_estimate=pl.CostEstimate(
             flops=2 * n_cols * (4 * feats * hidden + 3 * hidden * hidden + 2 * waves2 * feats),
             bytes_accessed=12 << 20,
             transcendentals=2 * n_cols * hidden,
         ),
-    )(gauss, bands, cot, *fixed)
-
-
-def to_spectral_kernel(group, place_ref, leg_ref, *refs):
-    ins, out_ref, hold = refs[:-2], refs[-2], refs[-1]
-    block, step = pl.program_id(0), pl.program_id(1)
-    per_step, degrees, lats = leg_ref.shape
+    )(gauss, bands, in_hbm(cot), *[in_hbm(a) for a in fixed])
+
+
+def to_spectral_kernel(
+    per_step, place_ref, leg_ref, early_ref, late_ref, after_ref, out_ref,
+    leg, early, late, hold, out, leg_sem, early_sem, late_sem, out_sem,
+):
+    del after_ref
+    waves, degrees, lats = leg_ref.shape
     feats = out_ref.shape[2]
-
-    @pl.when(step == 0)
-    def _():
-        peers, chunk_lats = ins[0].shape[0], ins[0].shape[1]
-        own = chunk_lats * len(ins)
-
-        def move(p, carry):
-            for c, source in enumerate(ins):
-                start = pl.multiple_of((p * own + c * chunk_lats) * group, group)
-                rows = source[pl.ds(p, 1)].reshape(chunk_lats * group, 2 * feats)
-                hold[pl.ds(start, chunk_lats * group), :] = rows.astype(F32)
-            return carry
-
-        lax.fori_loop(0, peers, move, 0)
-
-    for k in range(per_step):
-        place = step * per_step + k
-        wave = place_ref[0] + block * group + place
-        rows = hold[pl.ds(place, lats, stride=group), :].astype(BF16)
-        sums = jnp.dot(leg_ref[k], rows, preferred_element_type=F32).T
-        degree = lax.broadcasted_iota(jnp.int32, sums.shape, 1)
-        sums = jnp.where(degree >= wave, sums, 0.0)
-        out_ref[:, k] = sums.reshape(2, feats, degrees)
-
-
-def to_spectral(place, legendre, bands, chunk_lats):
+    _, peers, chunk_lats, width = early_ref.shape
+    steps = waves // per_step
+
+    def copies(step):
+        here = pl.ds(step * per_step, per_step)
+        return [
+            pltpu.make_async_copy(leg_ref.at[here], leg.at[here], leg_sem.at[step]),
+            pltpu.make_async_copy(early_ref.at[here], early.at[here], early_sem.at[step]),
+        ]
+
+    def send(step):
+        here = pl.ds(step * per_step, per_step)
+        return pltpu.make_async_copy(out.at[:, here], out_ref.at[:, here], out_sem.at[step])
+
+    first = pltpu.make_async_copy(late_ref.at[:, pl.ds(0, late.shape[1])], late, late_sem)
+    first.start()
+    for step in range(steps):
+        for copy in copies(step):
+            copy.start()
+    first.wait()
+
+    def move(p, carry):
+        start = pl.multiple_of(p * chunk_lats * waves, waves)
+        rows = late[pl.ds(p, 1)].reshape(chunk_lats * waves, width)
+        hold[pl.ds(start, chunk_lats * waves), :] = rows.astype(F32)
+        return carry
+
+    lax.fori_loop(0, peers, move, 0)
+
+    def work(step, carry):
+        for copy in copies(step):
+            copy.wait()
+        for k in range(per_step):
+            own_wave = step * per_step + k
+            second = hold[pl.ds(own_wave, peers * chunk_lats, stride=waves), :]
+            second = second.reshape(peers, chunk_lats, width)
+            rows = jnp.concatenate([early[own_wave].astype(F32), second], axis=1)
+            rows = rows.reshape(lats, width).astype(BF16)
+            sums = jnp.dot(leg[own_wave], rows, preferred_element_type=F32).T
+            degree = lax.broadcasted_iota(jnp.int32, sums.shape, 1)
+            sums = jnp.where(degree >= place_ref[0] + own_wave, sums, 0.0)
+            out[:, own_wave] = sums.reshape(2, feats, degrees)
+        send(step).start()
+        return carry
+
+    lax.fori_loop(0, steps, work, 0)
+    for step in range(steps):
+        send(step).wait()
+
+
+def to_spectral(place, legendre, early, late, after):
     waves, degrees, lats = legendre.shape
-    peers, _, _, width = bands[0].shape
+    _, peers, chunk_lats, width = early.shape
     feats = width // 2
-    group, per_step = min(16, waves), 8
-    steps = group // per_step
-    block = (peers, chunk_lats, group, width)
+    per_step, rows = min(16, waves), late.shape[2]
+    steps = waves // per_step
     return pl.pallas_call(
-        functools.partial(to_spectral_kernel, group),
-        grid=(waves // group, steps),
-        in_specs=[
-            pl.BlockSpec(memory_space=pltpu.SMEM),
-            pl.BlockSpec((per_step, degrees, lats), lambda b, s: (b * steps + s, 0, 0)),
-        ]
-        + [pl.BlockSpec(block, lambda b, s: (0, 0, b, 0))] * len(bands),
-        out_specs=pl.BlockSpec(
-            (2, per_step, feats, degrees), lambda b, s: (0, b * steps + s, 0, 0)
-        ),
+        functools.partial(to_spectral_kernel, per_step),
+        in_specs=[pl.BlockSpec(memory_space=pltpu.SMEM)] + [pl.BlockSpec(memory_space=pl.ANY)] * 4,
+        out_specs=pl.BlockSpec(memory_space=pl.ANY),
         out_shape=jax.ShapeDtypeStruct((2, waves, feats, degrees), F32),
-        scratch_shapes=[pltpu.VMEM((lats * group, width), F32)],
+        scratch_shapes=[
+            pltpu.VMEM(legendre.shape, BF16),
+            pltpu.VMEM(early.shape, BF16),
+            pltpu.VMEM((peers, chunk_lats * waves // rows, rows, width), BF16),
+            pltpu.VMEM((peers * chunk_lats * waves, width), F32),
+            pltpu.VMEM((2, waves, feats, degrees), F32),
+            pltpu.SemaphoreType.DMA((steps,)),
+            pltpu.SemaphoreType.DMA((steps,)),
+            pltpu.SemaphoreType.DMA,
+            pltpu.SemaphoreType.DMA((steps,)),
+        ],
         compiler_params=params(60),
         cost_estimate=pl.CostEstimate(
             flops=4 * waves * feats * degrees * lats, bytes_accessed=28 << 20, transcendentals=0
         ),
-    )(place, legendre, *bands)
+    )(place, legendre, early, late, after)
+
+
+def by_wave_kernel(in_ref, after_ref, out_ref, hold):
+    del after_ref
+    peers, lats, group, width = in_ref.shape
+
+    def move(p, carry):
+        start = pl.multiple_of(p * lats * group, group)
+        rows = in_ref[pl.ds(p, 1)].reshape(lats * group, width)
+        hold[pl.ds(start, lats * group), :] = rows.astype(F32)
+        return carry
+
+    lax.fori_loop(0, peers, move, 0)
+    for place in range(group):
+        rows = hold[pl.ds(place, peers * lats, stride=group), :]
+        out_ref[place] = rows.astype(BF16).reshape(peers, lats, width)
+
+
+def by_wave(values, after):
+    peers, lats, waves, width = values.shape
+    group = min(16, waves)
+    return pl.pallas_call(
+        by_wave_kernel,
+        grid=(waves // group,),
+        in_specs=[
+            pl.BlockSpec((peers, lats, group, width), lambda b: (0, 0, b, 0)),
+            pl.BlockSpec(memory_space=pl.ANY),
+        ],
+        out_specs=pl.BlockSpec((group, peers, lats, width), lambda b: (b, 0, 0, 0)),
+        out_shape=jax.ShapeDtypeStruct((waves, peers, lats, width), BF16),
+        scratch_shapes=[pltpu.VMEM((peers * lats * group, width), F32)],
+        compiler_params=params(60),
+        cost_estimate=pl.CostEstimate(flops=0, bytes_accessed=8 << 20, transcendentals=0),
+    )(values, after)
 
 
 def exchange(values):
     return lax.all_to_all(values, AXES, split_axis=0, concat_axis=0, tiled=True)
 
 
-def sum_over_lev(values, n_lev):
-    me = lax.axis_index("lev")
-    half = n_lev // 2
+def sum_over(axis, size, count, values):
+    me = lax.axis_index(axis)
+    half = count // 2
     while half:
         upper = jnp.where(me & half != 0, half, 0)
         kept = lax.dynamic_slice_in_dim(values, upper, half, axis=0)
         sent = lax.dynamic_slice_in_dim(values, half - upper, half, axis=0)
-        values = kept + lax.ppermute(sent, "lev", [(i, i ^ half) for i in range(n_lev)])
+        values = kept + lax.ppermute(sent, axis, [(i, i ^ half) for i in range(size)])
         half //= 2
     return values[0]
 
@@ -289,7 +389,6 @@
     lats = own_lats // 2
     lat, lev = lax.axis_index("lat"), lax.axis_index("lev")
     place = (lat * own_waves).astype(jnp.int32).reshape(1)
-    gauss = lax.dynamic_slice(gauss_weights, ((lat * n_lev + lev) * own_lats,), (own_lats,))
     table = basis_table(own_waves * n_lat, nlon)
     basis, basis_t = jnp.asarray(table), jnp.asarray(np.ascontiguousarray(table.T))
     tables = (basis, basis_t, w_first, w_second, w_third)
@@ -298,27 +397,36 @@
 
     shape = (n_lat, n_lev, lats, own_waves, width)
     one, two = [exchange(x) for x in to_fourier(place, spec, legendre, peers, 2)]
+    gauss = lax.dynamic_slice(gauss_weights, ((lat * n_lev + lev) * own_lats,), (own_lats,))
     sums = jnp.zeros((n_sums // feats, feats), F32)
-    back_one, sums = columns(gauss[:lats], one.reshape(shape), cotangent, 0, *tables, sums)
+    back_one, sums = columns(gauss[:lats], in_hbm(one.reshape(shape)), cotangent, 0, *tables, sums)
     back_one = exchange(back_one.reshape(one.shape))
     back_two, sums = columns(gauss[lats:], two.reshape(shape), cotangent, lats, *tables, sums)
 
-    sums = sum_over_lev(sums.reshape(n_lev, -1, feats), n_lev).reshape(peers, -1)
+    near = 2
+    sums = sum_over("lev", n_lev, n_lev, sums.reshape(n_lev, -1, feats))
+    sums = sum_over("lat", n_lat, near, sums.reshape(near, -1, feats)).reshape(peers, -1)
     size = sums.shape[1]
     pairs = split_values(sums).reshape(peers, -1)
-    unit = own_waves * width
-    pairs = jnp.pad(pairs, ((0, 0), (0, -pairs.shape[1] % unit)))
-    pairs = pairs.reshape(peers, -1, own_waves, width)
-    back_two = jnp.concatenate([back_two.reshape(two.shape), pairs], axis=1)
-    back_one, back_two = lax.optimization_barrier((back_one, back_two))
+    rows = min(16, own_waves)
+    pairs = jnp.pad(pairs, ((0, 0), (0, -pairs.shape[1] % (rows * width))))
+    pairs = pairs.reshape(peers, -1, rows, width)
+    back_two = back_two.reshape(peers, -1, rows, width)
+    units = back_two.shape[1]
+    back_two = jnp.concatenate([back_two, pairs], axis=1)
+    back_two, flag = lax.optimization_barrier((back_two, back_one[0, 0]))
     back_two = exchange(back_two)
-    pairs = back_two[:, lats:].reshape(n_lat, n_lev, -1)[:, :, : 2 * size]
-    pairs = pairs.reshape(n_lat, n_lev, 2, size).astype(F32)
-    share = pairs.sum(axis=(0, 2)) * (1.0 / math.sqrt(gauss_weights.shape[0] * nlon))
-    every = exchange(jnp.broadcast_to(share[None], (peers, n_lev, size)))
-    every = jnp.swapaxes(every, 0, 1).reshape(-1, feats)
-
-    out = to_spectral(place, legendre, [back_one, back_two], lats)
+    pairs = back_two[:, units:].reshape(n_lat // near, near, n_lev, -1)[..., : 2 * size]
+    pairs = pairs.reshape(n_lat // near, near, n_lev, 2, size).astype(F32)
+    share = pairs.sum(axis=(0, 3)) * (1.0 / math.sqrt(gauss_weights.shape[0] * nlon))
+    share = jnp.swapaxes(share, 0, 1)
+    early = by_wave(back_one, flag)
+    share, flag = lax.optimization_barrier((share, early[0, 0]))
+    share = share.astype(BF16)
+    every = exchange(jnp.broadcast_to(share[None], (peers,) + share.shape)).astype(F32)
+    every = jnp.moveaxis(every, 0, 2).reshape(-1, feats)
+
+    out = to_spectral(place, legendre, early, back_two, flag)
     halves = hidden // feats
     first, second = every[: halves * feats], every[halves * feats : halves * (feats + hidden)]
     grad_first = jnp.concatenate(jnp.split(first, halves), axis=1)

time: 255 us -> 249 us (0.976)
  blocking collectives: 114 us -> 56.1 us
  waiting for transfers between devices: 35.1 us -> 83.2 us
  starting transfers between devices: 12.6 us -> 16.7 us
    all_to_all x2 -> x1, blocking collectives: 114 us -> 56.1 us  [exchange(): return lax.all_to_all(values, AXES, split_axis=0, concat_axis=0, tiled=True)]
    all_to_all x3 -> x4, waiting for transfers between devices: 27 us -> 73.5 us  [exchange(): return lax.all_to_all(values, AXES, split_axis=0, concat_axis=0, tiled=True)]
    all_to_all x3 -> x4, starting transfers between devices: 11 us -> 15 us  [exchange(): return lax.all_to_all(values, AXES, split_axis=0, concat_axis=0, tiled=True)]
    squeeze x0 -> x2, local copies, waits for them, and re-layouts: none -> 2.55 us  [the longest x1 1.3 us: shards(): back_two, flag = lax.optimization_barrier((back_two, back_one[0, 0]))]
    pallas_call x2 -> x3, Pallas kernels: 25.1 us -> 26.8 us  [the longest x1 11.8 us: to_spectral(): pl.pallas_call(functools.partial(to_spectral_kernel, per_step), in_specs=...]
    ppermute x1 -> x2, waiting for transfers between devices: 8.11 us -> 9.66 us  [sum_over(): lax.ppermute(sent, axis, [(i, i ^ half) for i in range(size)])]
  transfers between devices with their start and end apart: 4 -> 6, of which waited for: 4 -> 5; matrix products, arithmetic and copies ran while one was open for 3% -> 2% of each run, Pallas kernels for 27% -> 28%
where the time goes in v3:
time: 249 us
  waiting for transfers between devices  83.2 us (33%)
  Pallas kernels  81.1 us (33%)
  blocking collectives  56.1 us (23%)
  starting transfers between devices  16.7 us (7%)
  local copies, waits for them, and re-layouts  6.7 us (3%)
  other arithmetic  3.9 us (2%)
    all_to_all x4, waiting for transfers between devices, exchange(): return lax.all_to_all(values, AXES, split_axis=0, concat_axis=0, tiled=True)  73.5 us
    all_to_all x1, blocking collectives, exchange(): return lax.all_to_all(values, AXES, split_axis=0, concat_axis=0, tiled=True)  56.1 us
    pallas_call x2, Pallas kernels, columns(): pl.pallas_call(columns_kernel, grid=(lats // per_step,), in_specs=[pl.Blo...  54.3 us
    all_to_all x4, starting transfers between devices, exchange(): return lax.all_to_all(values, AXES, split_axis=0, concat_axis=0, tiled=True)  15 us
    pallas_call x1, Pallas kernels, to_spectral(): pl.pallas_call(functools.partial(to_spectral_kernel, per_step), in_specs=...  11.8 us
    pallas_call x1, Pallas kernels, to_fourier(): pl.pallas_call(functools.partial(to_fourier_kernel, group, per_step), in_...  10.5 us
    ppermute x2, waiting for transfers between devices, sum_over(): lax.ppermute(sent, axis, [(i, i ^ half) for i in range(size)])  9.66 us
  transfers between devices with their start and end apart: 6, of which 5 were waited for; matrix products, arithmetic and copies ran while one was open for 2% of the time, Pallas kernels for 28%

profile of v3, /device:TPU:0, one launch (start us, length us, event | category | flops | bytes accessed | tf_op | source)
XLA Modules:
  0.0 248.5 jit_solution(3543583736813588564)
XLA Ops:
  0.6 10.5 %shard_map.120 = (bf16[32,8,32,128]{3,2,1,0:T(8,128)(2,1)}, bf16[32,8,32,128]{3,2,1,0:T(8,128)(2,1)}) custom-call(s32[1]{0:T(128)} %bitcast.place_ref, bf16[2,32,64,512]{3,2,1,0:T(8,128)(2,1)} %bitcast.26, bf16[32,512,512]{2,1,0:T(8,128)(2,1)} %leg_ref.3), custom_call_target="tpu_custom_call" | custom-call | flops 2147483648 | bytes 25165824 | tf_op jit(solution)/shard_map/pallas_call | solution.py:102
  11.2 56.1 %all_to_all.25 = bf16[32,8,32,128]{3,2,1,0:T(8,128)(2,1)} all-to-all(bf16[32,8,32,128]{3,2,1,0:T(8,128)(2,1)} %get-tuple-element.14), channel_id=1, replica_groups=mesh['lat'=16,'lev'=2] {'lat','lev'}, dimensions={0} | all-to-all | bytes 4194304 | tf_op jit(solution)/shard_map/all_to_all | solution.py:363
  67.3 3.7 %all-to-all-start.2 = ((bf16[32,8,32,128]{3,2,1,0:T(8,128)(2,1)}), bf16[32,8,32,128]{3,2,1,0:T(8,128)(2,1)S(1)}, u32[]{:S(2)}, u32[]{:S(2)}) async-start(bf16[32,8,32,128]{3,2,1,0:T(8,128)(2,1)} %get-tuple-element.16), calls=%async_computation.2 | async-start | bytes 4194304 | tf_op jit(solution)/shard_map/all_to_all | solution.py:363
  71.0 0.8 dynamic_slice.15
  71.8 0.1 fusion.2
  71.8 0.8 broadcast_in_dim.4.start_ref
  72.7 27.2 %shard_map.121 = (bf16[16,2,8,32,128]{4,3,2,1,0:T(8,128)(2,1)}, f32[1024,128]{1,0:T(8,128)S(1)}) custom-call(f32[8]{0:T(128)S(1)} %get-tuple-element.30.gauss_ref, bf16[16,2,8,32,128]{4,3,2,1,0:T(8,128)(2,1)} %bitcast.29, bf16[16,1024,128]{2,1,0:T(8,128)(2,1)} %cot_ref.3, bf16[1024,1024]{1,0:T(8,128)(2,1)} %constant.34.clone.basis_ref, ...), custom_call_target="tpu_custom_call" | custom-call | flops 9663676416 | bytes 12582912 | tf_op jit(solution)/shard_map/pallas_call | solution.py:210
  99.8 0.0 copy-start
  99.8 19.9 %all-to-all-done.2 = bf16[32,8,32,128]{3,2,1,0:T(8,128)(2,1)S(1)} async-done(((bf16[32,8,32,128]{3,2,1,0:T(8,128)(2,1)}), bf16[32,8,32,128]{3,2,1,0:T(8,128)(2,1)S(1)}, u32[]{:S(2)}, u32[]{:S(2)}) %all-to-all-start.2) | async-done | bytes 2097184 | tf_op jit(solution)/shard_map/all_to_all | solution.py:363
  119.7 0.0 copy-done
  119.7 4.0 %all-to-all-start.1 = ((bf16[32,8,32,128]{3,2,1,0:T(8,128)(2,1)}), bf16[32,8,32,128]{3,2,1,0:T(8,128)(2,1)}, u32[]{:S(2)}, u32[]{:S(2)}) async-start(bf16[32,8,32,128]{3,2,1,0:T(8,128)(2,1)} %bitcast.27), calls=%async_computation.1 | async-start | bytes 4194304 | tf_op jit(solution)/shard_map/all_to_all | solution.py:363
  123.7 27.1 %shard_map.122 = (bf16[16,2,8,32,128]{4,3,2,1,0:T(8,128)(2,1)}, f32[1024,128]{1,0:T(8,128)S(1)}) custom-call(f32[8]{0:T(128)S(1)} %get-tuple-element.29.gauss_ref, bf16[16,2,8,32,128]{4,3,2,1,0:T(8,128)(2,1)S(1)} %bitcast.22, bf16[16,1024,128]{2,1,0:T(8,128)(2,1)} %cot_ref.3, bf16[1024,1024]{1,0:T(8,128)(2,1)} %constant.34.clone.basis_ref, ...), custom_call_target="tpu_custom_call" | custom-call | flops 9663676416 | bytes 12582912 | tf_op jit(solution)/shard_map/pallas_call | solution.py:210
  150.9 0.0 copy-start.2
  150.9 1.6 collective-permute-start
  152.5 8.3 %collective-permute-done = f32[1,512,128]{2,1,0:T(8,128)S(1)} collective-permute-done((f32[1,512,128]{2,1,0:T(8,128)S(1)}, f32[1,512,128]{2,1,0:T(8,128)S(1)}, u32[]{:S(2)}, u32[]{:S(2)}) %collective-permute-start) | collective-permute-done | bytes 262176 | tf_op jit(solution)/shard_map/ppermute | solution.py:373
  160.9 0.1 collective-permute-start.1
  160.9 1.3 collective-permute-done.1
  162.3 0.1 convert_element_type.48
  162.4 0.1 subtract_convert_fusion
  162.5 0.3 pad_maximum_fusion.2
  162.8 0.1 reshape.75
  162.9 0.0 copy-done.2
  162.9 1.6 pad_maximum_fusion
  164.5 7.8 %all-to-all-done.1.in_ref = bf16[32,8,32,128]{3,2,1,0:T(8,128)(2,1)} async-done(((bf16[32,8,32,128]{3,2,1,0:T(8,128)(2,1)}), bf16[32,8,32,128]{3,2,1,0:T(8,128)(2,1)}, u32[]{:S(2)}, u32[]{:S(2)}) %all-to-all-start.1) | async-done | bytes 2097184 | tf_op jit(solution)/shard_map/all_to_all | solution.py:363
  172.2 1.3 slice_bitcast_fusion.after_ref
  173.5 3.7 %all-to-all-start.3 = ((bf16[32,17,16,128]{3,2,1,0:T(8,128)(2,1)}), bf16[32,17,16,128]{3,2,1,0:T(8,128)(2,1)S(1)}, u32[]{:S(2)}, u32[]{:S(2)}) async-start(bf16[32,17,16,128]{3,2,1,0:T(8,128)(2,1)} %pad_maximum_fusion), calls=%async_computation.3 | async-start | bytes 4456448 | tf_op jit(solution)/shard_map/all_to_all | solution.py:363
  177.2 4.5 %shard_map.123.early_ref = bf16[32,32,8,128]{3,2,1,0:T(8,128)(2,1)} custom-call(bf16[32,8,32,128]{3,2,1,0:T(8,128)(2,1)} %all-to-all-done.1.in_ref, bf16[32,128]{1,0:T(8,128)(2,1)} %slice_bitcast_fusion.after_ref), custom_call_target="tpu_custom_call" | custom-call | bytes 8388608 | tf_op jit(solution)/shard_map/pallas_call | solution.py:347
  181.7 1.3 slice_bitcast_fusion.1.after_ref
  182.9 45.8 %all-to-all-done.3.late_ref = bf16[32,17,16,128]{3,2,1,0:T(8,128)(2,1)S(1)} async-done(((bf16[32,17,16,128]{3,2,1,0:T(8,128)(2,1)}), bf16[32,17,16,128]{3,2,1,0:T(8,128)(2,1)S(1)}, u32[]{:S(2)}, u32[]{:S(2)}) %all-to-all-start.3) | async-done | bytes 2228256 | tf_op jit(solution)/shard_map/all_to_all | solution.py:363
  228.8 0.0 copy-start.1
  228.8 0.1 reshape.78
  229.0 0.1 reduce_sum.9
  229.1 1.1 broadcast_in_dim.10
  230.2 3.7 %all-to-all-start.4 = ((bf16[32,2,2,1024]{3,2,1,0:T(2,128)(2,1)}), bf16[32,2,2,1024]{3,2,1,0:T(2,128)(2,1)S(1)}, u32[]{:S(2)}, u32[]{:S(2)}) async-start(bf16[32,2,2,1024]{3,2,1,0:T(2,128)(2,1)} %broadcast_in_dim.10), calls=%async_computation.4 | async-start | bytes 524288 | tf_op jit(solution)/shard_map/all_to_all | solution.py:363
  233.9 0.0 copy-done.1
  233.9 11.8 %shard_map.124 = f32[2,32,64,512]{3,2,1,0:T(8,128)} custom-call(s32[1]{0:T(128)} %bitcast.place_ref, bf16[32,512,512]{2,1,0:T(8,128)(2,1)} %leg_ref.3, bf16[32,32,8,128]{3,2,1,0:T(8,128)(2,1)} %shard_map.123.early_ref, bf16[32,17,16,128]{3,2,1,0:T(8,128)(2,1)} %copy-done.1, bf16[8,128]{1,0:T(8,128)(2,1)} %slice_bitcast_fusion.1.after_ref), custom_call_target="tpu_custom_call" | custom-call | flops 2147483648 | bytes 29360128 | tf_op jit(solution)/shard_map/pallas_call | solution.py:305
  245.7 0.0 all-to-all-done.4
  245.8 0.3 convert_bitcast_fusion
  246.0 0.3 copy.15
  246.4 0.1 reshape.80
  246.5 0.7 fusion
  247.2 0.7 pad_maximum_fusion.3
  247.8 0.7 pad_maximum_fusion.1
  (8 shorter events, 0.1 us)
Async XLA Ops:
  67.3 52.4 %all-to-all-start.2 = ((bf16[32,8,32,128]{3,2,1,0:T(8,128)(2,1)}), bf16[32,8,32,128]{3,2,1,0:T(8,128)(2,1)S(1)}, u32[]{:S(2)}, u32[]{:S(2)}) async-start(bf16[32,8,32,128]{3,2,1,0:T(8,128)(2,1)} %get-tuple-element.16), calls=%async_computation.2 | async-start | bytes 4194304 | tf_op jit(solution)/shard_map/all_to_all | solution.py:363
  99.8 19.9 %copy-start = (f32[1024,128]{1,0:T(8,128)}, f32[1024,128]{1,0:T(8,128)S(1)}, u32[]{:S(2)}) copy-start(f32[1024,128]{1,0:T(8,128)S(1)} %get-tuple-element.17.start_ref) | copy-start | bytes 1572868
  119.7 52.5 %all-to-all-start.1 = ((bf16[32,8,32,128]{3,2,1,0:T(8,128)(2,1)}), bf16[32,8,32,128]{3,2,1,0:T(8,128)(2,1)}, u32[]{:S(2)}, u32[]{:S(2)}) async-start(bf16[32,8,32,128]{3,2,1,0:T(8,128)(2,1)} %bitcast.27), calls=%async_computation.1 | async-start | bytes 4194304 | tf_op jit(solution)/shard_map/all_to_all | solution.py:363
  150.9 12.0 %copy-start.2 = (bf16[16,2,8,32,128]{4,3,2,1,0:T(8,128)(2,1)S(1)}, bf16[16,2,8,32,128]{4,3,2,1,0:T(8,128)(2,1)}, u32[]{:S(2)}) copy-start(bf16[16,2,8,32,128]{4,3,2,1,0:T(8,128)(2,1)} %get-tuple-element.18) | copy-start | bytes 6291460
  150.9 9.9 %collective-permute-start = (f32[1,512,128]{2,1,0:T(8,128)S(1)}, f32[1,512,128]{2,1,0:T(8,128)S(1)}, u32[]{:S(2)}, u32[]{:S(2)}) collective-permute-start(f32[1,512,128]{2,1,0:T(8,128)S(1)} %constant_dynamic-slice_fusion.1), channel_id=1, source_target_pairs={{0,1},{1,0},{2,3},{3,2},{4,5},{5,4},{6,7},{7,6},{8,9},{9,8},{10,11... | collective-permute-start | bytes 786440 | tf_op jit(solution)/shard_map/ppermute | solution.py:373
  160.9 1.4 collective-permute-start.1
  173.5 55.3 %all-to-all-start.3 = ((bf16[32,17,16,128]{3,2,1,0:T(8,128)(2,1)}), bf16[32,17,16,128]{3,2,1,0:T(8,128)(2,1)S(1)}, u32[]{:S(2)}, u32[]{:S(2)}) async-start(bf16[32,17,16,128]{3,2,1,0:T(8,128)(2,1)} %pad_maximum_fusion), calls=%async_computation.3 | async-start | bytes 4456448 | tf_op jit(solution)/shard_map/all_to_all | solution.py:363
  228.8 5.1 %copy-start.1 = (bf16[32,17,16,128]{3,2,1,0:T(8,128)(2,1)}, bf16[32,17,16,128]{3,2,1,0:T(8,128)(2,1)S(1)}, u32[]{:S(2)}) copy-start(bf16[32,17,16,128]{3,2,1,0:T(8,128)(2,1)S(1)} %all-to-all-done.3.late_ref) | copy-start | bytes 6684676
  230.2 15.5 %all-to-all-start.4 = ((bf16[32,2,2,1024]{3,2,1,0:T(2,128)(2,1)}), bf16[32,2,2,1024]{3,2,1,0:T(2,128)(2,1)S(1)}, u32[]{:S(2)}, u32[]{:S(2)}) async-start(bf16[32,2,2,1024]{3,2,1,0:T(2,128)(2,1)} %broadcast_in_dim.10), calls=%async_computation.4 | async-start | bytes 524288 | tf_op jit(solution)/shard_map/all_to_all | solution.py:363

commit v4 on v3

--- a/solution.py
+++ b/solution.py
@@ -247,7 +247,7 @@
     waves, degrees, lats = leg_ref.shape
     feats = out_ref.shape[2]
     _, peers, chunk_lats, width = early_ref.shape
-    steps = waves // per_step
+    steps, per_send = waves // per_step, min(4, per_step)
 
     def copies(step):
         here = pl.ds(step * per_step, per_step)
@@ -257,7 +257,7 @@
         ]
 
     def send(step):
-        here = pl.ds(step * per_step, per_step)
+        here = pl.ds(step * per_send, per_send)
         return pltpu.make_async_copy(out.at[:, here], out_ref.at[:, here], out_sem.at[step])
 
     first = pltpu.make_async_copy(late_ref.at[:, pl.ds(0, late.shape[1])], late, late_sem)
@@ -288,11 +288,12 @@
             degree = lax.broadcasted_iota(jnp.int32, sums.shape, 1)
             sums = jnp.where(degree >= place_ref[0] + own_wave, sums, 0.0)
             out[:, own_wave] = sums.reshape(2, feats, degrees)
-        send(step).start()
+            if k % per_send == per_send - 1:
+                send(step * (per_step // per_send) + k // per_send).start()
         return carry
 
     lax.fori_loop(0, steps, work, 0)
-    for step in range(steps):
+    for step in range(waves // per_send):
         send(step).wait()
 
 
@@ -316,7 +317,7 @@
             pltpu.SemaphoreType.DMA((steps,)),
             pltpu.SemaphoreType.DMA((steps,)),
             pltpu.SemaphoreType.DMA,
-            pltpu.SemaphoreType.DMA((steps,)),
+            pltpu.SemaphoreType.DMA((waves // min(4, per_step),)),
         ],
         compiler_params=params(60),
         cost_estimate=pl.CostEstimate(
@@ -325,8 +326,7 @@
     )(place, legendre, early, late, after)
 
 
-def by_wave_kernel(in_ref, after_ref, out_ref, hold):
-    del after_ref
+def by_wave_kernel(in_ref, out_ref, hold):
     peers, lats, group, width = in_ref.shape
 
     def move(p, carry):
@@ -341,22 +341,19 @@
         out_ref[place] = rows.astype(BF16).reshape(peers, lats, width)
 
 
-def by_wave(values, after):
+def by_wave(values):
     peers, lats, waves, width = values.shape
     group = min(16, waves)
     return pl.pallas_call(
         by_wave_kernel,
         grid=(waves // group,),
-        in_specs=[
-            pl.BlockSpec((peers, lats, group, width), lambda b: (0, 0, b, 0)),
-            pl.BlockSpec(memory_space=pl.ANY),
-        ],
+        in_specs=[pl.BlockSpec((peers, lats, group, width), lambda b: (0, 0, b, 0))],
         out_specs=pl.BlockSpec((group, peers, lats, width), lambda b: (b, 0, 0, 0)),
         out_shape=jax.ShapeDtypeStruct((waves, peers, lats, width), BF16),
         scratch_shapes=[pltpu.VMEM((peers * lats * group, width), F32)],
         compiler_params=params(60),
         cost_estimate=pl.CostEstimate(flops=0, bytes_accessed=8 << 20, transcendentals=0),
-    )(values, after)
+    )(values)
 
 
 def exchange(values):
@@ -378,6 +375,40 @@
 def split_values(values):
     high = values.astype(BF16)
     return jnp.stack([high, (values - high.astype(F32)).astype(BF16)], axis=1)
+
+
+def gradients_kernel(rows, every_ref, first_ref, second_ref, third_ref, flat):
+    values = every_ref[...].astype(F32)
+    peers, count, feats = values.shape
+    for at in range(0, count, rows):
+        part = values[:, at : at + rows].reshape(peers * rows, feats)
+        flat[at * peers : (at + rows) * peers] = part
+    hidden = second_ref.shape[0]
+    halves = hidden // feats
+    for h in range(halves):
+        cols = slice(h * feats, (h + 1) * feats)
+        first_ref[:, cols] = flat[h * feats : (h + 1) * feats]
+        second_ref[:, cols] = flat[(h + 1) * hidden : (h + 2) * hidden]
+    third_ref[...] = flat[(halves + 1) * hidden :]
+
+
+def gradients(every, rows, feats, hidden):
+    halves = hidden // feats
+    shapes = [(feats, hidden), (hidden, hidden), (hidden, feats)]
+    total = halves * (feats + hidden) + hidden
+    if every.ndim == 3:
+        return pl.pallas_call(
+            functools.partial(gradients_kernel, rows),
+            out_shape=[jax.ShapeDtypeStruct(shape, F32) for shape in shapes],
+            scratch_shapes=[pltpu.VMEM((total, feats), F32)],
+        )(every)
+    flat = jnp.moveaxis(every.astype(F32), 0, 2).reshape(-1, feats)
+    first, second = flat[: halves * feats], flat[halves * feats : halves * (feats + hidden)]
+    return (
+        jnp.concatenate(jnp.split(first, halves), axis=1),
+        jnp.concatenate(jnp.split(second, halves), axis=1),
+        flat[halves * (feats + hidden) :],
+    )
 
 
 def shards(n_lat, n_lev, spectral, legendre, gauss_weights, w_first, w_second, w_third, cotangent):
@@ -414,25 +445,22 @@
     back_two = back_two.reshape(peers, -1, rows, width)
     units = back_two.shape[1]
     back_two = jnp.concatenate([back_two, pairs], axis=1)
-    back_two, flag = lax.optimization_barrier((back_two, back_one[0, 0]))
+    back_one, back_two = lax.optimization_barrier((back_one, back_two))
     back_two = exchange(back_two)
     pairs = back_two[:, units:].reshape(n_lat // near, near, n_lev, -1)[..., : 2 * size]
     pairs = pairs.reshape(n_lat // near, near, n_lev, 2, size).astype(F32)
     share = pairs.sum(axis=(0, 3)) * (1.0 / math.sqrt(gauss_weights.shape[0] * nlon))
     share = jnp.swapaxes(share, 0, 1)
-    early = by_wave(back_one, flag)
+    early = by_wave(back_one)
     share, flag = lax.optimization_barrier((share, early[0, 0]))
     share = share.astype(BF16)
-    every = exchange(jnp.broadcast_to(share[None], (peers,) + share.shape)).astype(F32)
-    every = jnp.moveaxis(every, 0, 2).reshape(-1, feats)
+    if size % (8 * feats) == 0:
+        share = share.reshape(-1, feats)
+    every = exchange(jnp.broadcast_to(share[None], (peers,) + share.shape))
 
     out = to_spectral(place, legendre, early, back_two, flag)
-    halves = hidden // feats
-    first, second = every[: halves * feats], every[halves * feats : halves * (feats + hidden)]
-    grad_first = jnp.concatenate(jnp.split(first, halves), axis=1)
-    grad_second = jnp.concatenate(jnp.split(second, halves), axis=1)
-    grad_third = every[halves * (feats + hidden) :]
-    return (jnp.swapaxes(out, 2, 3), grad_first, grad_second, grad_third)
+    grads = gradients(every, size // feats, feats, hidden)
+    return (jnp.swapaxes(out, 2, 3), *grads)
 
 
 def solution(mesh):

time: 249 us -> 247 us (level)
  no operation moved by 1% of the time
where the time goes in v4:
time: 247 us; the launch traced here: 246 us
  waiting for transfers between devices  83.2 us (34%)
  Pallas kernels  82.2 us (33%)
  blocking collectives  56.1 us (23%)
  starting transfers between devices  16.7 us (7%)
  local copies, waits for them, and re-layouts  4.94 us (2%)
    all_to_all x4, waiting for transfers between devices, exchange(): return lax.all_to_all(values, AXES, split_axis=0, concat_axis=0, tiled=True)  73.5 us
    all_to_all x1, blocking collectives, exchange(): return lax.all_to_all(values, AXES, split_axis=0, concat_axis=0, tiled=True)  56.1 us
    pallas_call x2, Pallas kernels, columns(): pl.pallas_call(columns_kernel, grid=(lats // per_step,), in_specs=[pl.Blo...  54.3 us
    all_to_all x4, starting transfers between devices, exchange(): return lax.all_to_all(values, AXES, split_axis=0, concat_axis=0, tiled=True)  15 us
    pallas_call x1, Pallas kernels, to_spectral(): pl.pallas_call(functools.partial(to_spectral_kernel, per_step), in_specs=...  11.2 us
    pallas_call x1, Pallas kernels, to_fourier(): pl.pallas_call(functools.partial(to_fourier_kernel, group, per_step), in_...  10.5 us
    ppermute x2, waiting for transfers between devices, sum_over(): lax.ppermute(sent, axis, [(i, i ^ half) for i in range(size)])  9.66 us
  transfers between devices with their start and end apart: 6, of which 5 were waited for; matrix products, arithmetic and copies ran while one was open for 2% of the time, Pallas kernels for 28%

profile of v4, /device:TPU:0, one launch (start us, length us, event | category | flops | bytes accessed | tf_op | source)
XLA Modules:
  0.0 246.2 jit_solution(5675957888625612402)
XLA Ops:
  0.6 10.5 %shard_map.120 = (bf16[32,8,32,128]{3,2,1,0:T(8,128)(2,1)}, bf16[32,8,32,128]{3,2,1,0:T(8,128)(2,1)}) custom-call(s32[1]{0:T(128)} %bitcast.place_ref, bf16[2,32,64,512]{3,2,1,0:T(8,128)(2,1)} %bitcast.20, bf16[32,512,512]{2,1,0:T(8,128)(2,1)} %leg_ref.3), custom_call_target="tpu_custom_call" | custom-call | flops 2147483648 | bytes 25165824 | tf_op jit(solution)/shard_map/pallas_call | solution.py:102
  11.2 56.1 %all_to_all.25 = bf16[32,8,32,128]{3,2,1,0:T(8,128)(2,1)} all-to-all(bf16[32,8,32,128]{3,2,1,0:T(8,128)(2,1)} %get-tuple-element.17), channel_id=1, replica_groups=mesh['lat'=16,'lev'=2] {'lat','lev'}, dimensions={0} | all-to-all | bytes 4194304 | tf_op jit(solution)/shard_map/all_to_all | solution.py:360
  67.3 3.7 %all-to-all-start.2 = ((bf16[32,8,32,128]{3,2,1,0:T(8,128)(2,1)}), bf16[32,8,32,128]{3,2,1,0:T(8,128)(2,1)S(1)}, u32[]{:S(2)}, u32[]{:S(2)}) async-start(bf16[32,8,32,128]{3,2,1,0:T(8,128)(2,1)} %get-tuple-element.19), calls=%async_computation.2 | async-start | bytes 4194304 | tf_op jit(solution)/shard_map/all_to_all | solution.py:360
  71.0 0.8 dynamic_slice.15
  71.8 0.1 fusion
  71.8 0.8 broadcast_in_dim.10.start_ref
  72.7 27.2 %shard_map.121 = (bf16[16,2,8,32,128]{4,3,2,1,0:T(8,128)(2,1)}, f32[1024,128]{1,0:T(8,128)S(1)}) custom-call(f32[8]{0:T(128)S(1)} %get-tuple-element.31.gauss_ref, bf16[16,2,8,32,128]{4,3,2,1,0:T(8,128)(2,1)} %bitcast.23, bf16[16,1024,128]{2,1,0:T(8,128)(2,1)} %cot_ref.3, bf16[1024,1024]{1,0:T(8,128)(2,1)} %constant.34.clone.basis_ref, ...), custom_call_target="tpu_custom_call" | custom-call | flops 9663676416 | bytes 12582912 | tf_op jit(solution)/shard_map/pallas_call | solution.py:210
  99.8 0.0 copy-start
  99.8 19.9 %all-to-all-done.2 = bf16[32,8,32,128]{3,2,1,0:T(8,128)(2,1)S(1)} async-done(((bf16[32,8,32,128]{3,2,1,0:T(8,128)(2,1)}), bf16[32,8,32,128]{3,2,1,0:T(8,128)(2,1)S(1)}, u32[]{:S(2)}, u32[]{:S(2)}) %all-to-all-start.2) | async-done | bytes 2097184 | tf_op jit(solution)/shard_map/all_to_all | solution.py:360
  119.7 0.0 copy-done
  119.7 4.0 %all-to-all-start.1 = ((bf16[32,8,32,128]{3,2,1,0:T(8,128)(2,1)}), bf16[32,8,32,128]{3,2,1,0:T(8,128)(2,1)}, u32[]{:S(2)}, u32[]{:S(2)}) async-start(bf16[32,8,32,128]{3,2,1,0:T(8,128)(2,1)} %bitcast.21), calls=%async_computation.1 | async-start | bytes 4194304 | tf_op jit(solution)/shard_map/all_to_all | solution.py:360
  123.7 27.1 %shard_map.122 = (bf16[16,2,8,32,128]{4,3,2,1,0:T(8,128)(2,1)}, f32[1024,128]{1,0:T(8,128)S(1)}) custom-call(f32[8]{0:T(128)S(1)} %get-tuple-element.30.gauss_ref, bf16[16,2,8,32,128]{4,3,2,1,0:T(8,128)(2,1)S(1)} %bitcast.16, bf16[16,1024,128]{2,1,0:T(8,128)(2,1)} %cot_ref.3, bf16[1024,1024]{1,0:T(8,128)(2,1)} %constant.34.clone.basis_ref, ...), custom_call_target="tpu_custom_call" | custom-call | flops 9663676416 | bytes 12582912 | tf_op jit(solution)/shard_map/pallas_call | solution.py:210
  150.9 0.0 copy-start.2
  150.9 1.6 collective-permute-start
  152.5 8.3 %collective-permute-done = f32[1,512,128]{2,1,0:T(8,128)S(1)} collective-permute-done((f32[1,512,128]{2,1,0:T(8,128)S(1)}, f32[1,512,128]{2,1,0:T(8,128)S(1)}, u32[]{:S(2)}, u32[]{:S(2)}) %collective-permute-start) | collective-permute-done | bytes 262176 | tf_op jit(solution)/shard_map/ppermute | solution.py:370
  160.9 0.1 collective-permute-start.1
  160.9 1.3 collective-permute-done.1
  162.3 0.1 convert_element_type.47
  162.4 0.1 subtract_convert_fusion
  162.5 0.3 pad_maximum_fusion.1
  162.8 0.1 reshape.69
  162.9 0.0 copy-done.2
  162.9 1.6 pad_maximum_fusion
  164.5 7.8 %all-to-all-done.1.in_ref = bf16[32,8,32,128]{3,2,1,0:T(8,128)(2,1)} async-done(((bf16[32,8,32,128]{3,2,1,0:T(8,128)(2,1)}), bf16[32,8,32,128]{3,2,1,0:T(8,128)(2,1)}, u32[]{:S(2)}, u32[]{:S(2)}) %all-to-all-start.1) | async-done | bytes 2097184 | tf_op jit(solution)/shard_map/all_to_all | solution.py:360
  172.2 3.7 %all-to-all-start.3 = ((bf16[32,17,16,128]{3,2,1,0:T(8,128)(2,1)}), bf16[32,17,16,128]{3,2,1,0:T(8,128)(2,1)S(1)}, u32[]{:S(2)}, u32[]{:S(2)}) async-start(bf16[32,17,16,128]{3,2,1,0:T(8,128)(2,1)} %pad_maximum_fusion), calls=%async_computation.3 | async-start | bytes 4456448 | tf_op jit(solution)/shard_map/all_to_all | solution.py:360
  175.9 4.5 %shard_map.123.early_ref = bf16[32,32,8,128]{3,2,1,0:T(8,128)(2,1)} custom-call(bf16[32,8,32,128]{3,2,1,0:T(8,128)(2,1)} %all-to-all-done.1.in_ref), custom_call_target="tpu_custom_call" | custom-call | bytes 8388608 | tf_op jit(solution)/shard_map/pallas_call | solution.py:347
  180.4 1.3 slice_bitcast_fusion.after_ref
  181.7 45.8 %all-to-all-done.3.late_ref = bf16[32,17,16,128]{3,2,1,0:T(8,128)(2,1)S(1)} async-done(((bf16[32,17,16,128]{3,2,1,0:T(8,128)(2,1)}), bf16[32,17,16,128]{3,2,1,0:T(8,128)(2,1)S(1)}, u32[]{:S(2)}, u32[]{:S(2)}) %all-to-all-start.3) | async-done | bytes 2228256 | tf_op jit(solution)/shard_map/all_to_all | solution.py:360
  227.5 0.0 copy-start.1
  227.5 0.1 reshape.70
  227.7 0.1 reduce_sum.9
  227.8 1.0 broadcast_in_dim.12
  228.9 3.7 %all-to-all-start.4 = ((bf16[32,32,128]{2,1,0:T(8,128)(2,1)}), bf16[32,32,128]{2,1,0:T(8,128)(2,1)S(1)}, u32[]{:S(2)}, u32[]{:S(2)}) async-start(bf16[32,32,128]{2,1,0:T(8,128)(2,1)} %broadcast_in_dim.12), calls=%async_computation.4 | async-start | bytes 524288 | tf_op jit(solution)/shard_map/all_to_all | solution.py:360
  232.5 0.0 copy-done.1
  232.5 11.2 %shard_map.124 = f32[2,32,64,512]{3,2,1,0:T(8,128)} custom-call(s32[1]{0:T(128)} %bitcast.place_ref, bf16[32,512,512]{2,1,0:T(8,128)(2,1)} %leg_ref.3, bf16[32,32,8,128]{3,2,1,0:T(8,128)(2,1)} %shard_map.123.early_ref, bf16[32,17,16,128]{3,2,1,0:T(8,128)(2,1)} %copy-done.1, bf16[8,128]{1,0:T(8,128)(2,1)} %slice_bitcast_fusion.after_ref), custom_call_target="tpu_custom_call" | custom-call | flops 2147483648 | bytes 29360128 | tf_op jit(solution)/shard_map/pallas_call | solution.py:306
  243.7 0.0 all-to-all-done.4.every_ref
  243.7 0.0 copy-start.3
  243.8 0.7 copy-done.3
  244.4 1.8 shard_map.125
  (8 shorter events, 0.1 us)
Async XLA Ops:
  67.3 52.4 %all-to-all-start.2 = ((bf16[32,8,32,128]{3,2,1,0:T(8,128)(2,1)}), bf16[32,8,32,128]{3,2,1,0:T(8,128)(2,1)S(1)}, u32[]{:S(2)}, u32[]{:S(2)}) async-start(bf16[32,8,32,128]{3,2,1,0:T(8,128)(2,1)} %get-tuple-element.19), calls=%async_computation.2 | async-start | bytes 4194304 | tf_op jit(solution)/shard_map/all_to_all | solution.py:360
  99.8 19.9 %copy-start = (f32[1024,128]{1,0:T(8,128)}, f32[1024,128]{1,0:T(8,128)S(1)}, u32[]{:S(2)}) copy-start(f32[1024,128]{1,0:T(8,128)S(1)} %get-tuple-element.20.start_ref) | copy-start | bytes 1572868
  119.7 52.5 %all-to-all-start.1 = ((bf16[32,8,32,128]{3,2,1,0:T(8,128)(2,1)}), bf16[32,8,32,128]{3,2,1,0:T(8,128)(2,1)}, u32[]{:S(2)}, u32[]{:S(2)}) async-start(bf16[32,8,32,128]{3,2,1,0:T(8,128)(2,1)} %bitcast.21), calls=%async_computation.1 | async-start | bytes 4194304 | tf_op jit(solution)/shard_map/all_to_all | solution.py:360
  150.9 12.0 %copy-start.2 = (bf16[16,2,8,32,128]{4,3,2,1,0:T(8,128)(2,1)S(1)}, bf16[16,2,8,32,128]{4,3,2,1,0:T(8,128)(2,1)}, u32[]{:S(2)}) copy-start(bf16[16,2,8,32,128]{4,3,2,1,0:T(8,128)(2,1)} %get-tuple-element.21) | copy-start | bytes 6291460
  150.9 9.9 %collective-permute-start = (f32[1,512,128]{2,1,0:T(8,128)S(1)}, f32[1,512,128]{2,1,0:T(8,128)S(1)}, u32[]{:S(2)}, u32[]{:S(2)}) collective-permute-start(f32[1,512,128]{2,1,0:T(8,128)S(1)} %constant_dynamic-slice_fusion.1), channel_id=1, source_target_pairs={{0,1},{1,0},{2,3},{3,2},{4,5},{5,4},{6,7},{7,6},{8,9},{9,8},{10,11... | collective-permute-start | bytes 786440 | tf_op jit(solution)/shard_map/ppermute | solution.py:370
  160.9 1.4 collective-permute-start.1
  172.2 55.3 %all-to-all-start.3 = ((bf16[32,17,16,128]{3,2,1,0:T(8,128)(2,1)}), bf16[32,17,16,128]{3,2,1,0:T(8,128)(2,1)S(1)}, u32[]{:S(2)}, u32[]{:S(2)}) async-start(bf16[32,17,16,128]{3,2,1,0:T(8,128)(2,1)} %pad_maximum_fusion), calls=%async_computation.3 | async-start | bytes 4456448 | tf_op jit(solution)/shard_map/all_to_all | solution.py:360
  227.5 5.0 %copy-start.1 = (bf16[32,17,16,128]{3,2,1,0:T(8,128)(2,1)}, bf16[32,17,16,128]{3,2,1,0:T(8,128)(2,1)S(1)}, u32[]{:S(2)}) copy-start(bf16[32,17,16,128]{3,2,1,0:T(8,128)(2,1)S(1)} %all-to-all-done.3.late_ref) | copy-start | bytes 6684676
  228.9 14.9 %all-to-all-start.4 = ((bf16[32,32,128]{2,1,0:T(8,128)(2,1)}), bf16[32,32,128]{2,1,0:T(8,128)(2,1)S(1)}, u32[]{:S(2)}, u32[]{:S(2)}) async-start(bf16[32,32,128]{2,1,0:T(8,128)(2,1)} %broadcast_in_dim.12), calls=%async_computation.4 | async-start | bytes 524288 | tf_op jit(solution)/shard_map/all_to_all | solution.py:360
  243.7 0.7 copy-start.3

commit v5 on v4

--- a/solution.py
+++ b/solution.py
@@ -32,9 +32,8 @@
 
 
 def to_fourier_kernel(group, per_step, place_ref, spec_ref, leg_ref, *refs):
-    chunks = (len(refs) - 6) // 2
-    outs, stages = refs[:chunks], refs[chunks : 2 * chunks]
-    spec, leg, hold, spec_sem, leg_sem, out_sem = refs[2 * chunks :]
+    chunks = len(refs) - 5
+    outs, (spec, leg, hold, spec_sem, leg_sem) = refs[:chunks], refs[chunks:]
     waves, degrees, lats = leg_ref.shape
     feats = spec_ref.shape[2]
     peers, chunk_lats = outs[0].shape[:2]
@@ -53,7 +52,6 @@
         return carry
 
     lax.fori_loop(0, waves // per_step, start, 0)
-    sends = []
     for block in range(waves // group):
 
         def work(step, carry):
@@ -76,19 +74,11 @@
             for c in range(chunks):
                 first = pl.multiple_of((p * own + c * chunk_lats) * group, group)
                 rows = hold[pl.ds(first, chunk_lats * group), :].astype(BF16)
-                rows = rows.reshape(1, 1, chunk_lats, group, 2 * feats)
-                stages[c][block : block + 1, pl.ds(p, 1)] = rows
+                rows = rows.reshape(1, chunk_lats, group, 2 * feats)
+                outs[c][pl.ds(p, 1), :, block * group : (block + 1) * group] = rows
             return carry
 
         lax.fori_loop(0, peers, move, 0)
-        for c in range(chunks):
-            there = outs[c].at[:, :, block * group : (block + 1) * group]
-            sends.append(
-                pltpu.make_async_copy(stages[c].at[block], there, out_sem.at[block, c])
-            )
-            sends[-1].start()
-    for send in sends:
-        send.wait()
 
 
 def to_fourier(place, spec, legendre, peers, chunks):
@@ -98,26 +88,23 @@
     per_step = min(4, group)
     chunk_lats = lats // peers // chunks
     shape = (peers, chunk_lats, waves, 2 * feats)
-    stage = (waves // group, peers, chunk_lats, group, 2 * feats)
     return pl.pallas_call(
         functools.partial(to_fourier_kernel, group, per_step),
         in_specs=[pl.BlockSpec(memory_space=pltpu.SMEM)] + [pl.BlockSpec(memory_space=pl.ANY)] * 2,
-        out_specs=[pl.BlockSpec(memory_space=pl.ANY)] * chunks,
-        out_shape=[jax.ShapeDtypeStruct(shape, BF16)] * chunks,
-        scratch_shapes=[pltpu.VMEM(stage, BF16)] * chunks
-        + [
+        out_specs=[pl.BlockSpec(memory_space=pltpu.VMEM)] * chunks,
+        out_shape=[pltpu.VMEM(shape, BF16)] * chunks,
+        scratch_shapes=[
             pltpu.VMEM(spec.shape, BF16),
             pltpu.VMEM(legendre.shape, BF16),
             pltpu.VMEM((lats * group, 2 * feats), F32),
             pltpu.SemaphoreType.DMA((waves // per_step,)),
             pltpu.SemaphoreType.DMA((waves // per_step,)),
-            pltpu.SemaphoreType.DMA((waves // group, chunks)),
         ],
-        compiler_params=params(60),
+        compiler_params=params(40),
         cost_estimate=pl.CostEstimate(
             flops=4 * waves * feats * degrees * lats, bytes_accessed=24 << 20, transcendentals=0
         ),
-    )(place, spec, legendre)
+    )(place, in_hbm(spec), in_hbm(legendre))
 
 
 def sigmoid(value):

time: 247 us -> 245 us (level)
  transfers between devices with their start and end apart: 6 -> 6, of which waited for: 5 -> 5; matrix products, arithmetic and copies ran while one was open for 2% -> 2% of each run, Pallas kernels for 28% -> 29%
where the time goes in v5:
time: 245 us
  waiting for transfers between devices  82.4 us (34%)
  Pallas kernels  80.8 us (33%)
  blocking collectives  55.9 us (23%)
  starting transfers between devices  16.7 us (7%)
  local copies, waits for them, and re-layouts  5.72 us (2%)
    all_to_all x4, waiting for transfers between devices, exchange(): return lax.all_to_all(values, AXES, split_axis=0, concat_axis=0, tiled=True)  72.8 us
    all_to_all x1, blocking collectives, exchange(): return lax.all_to_all(values, AXES, split_axis=0, concat_axis=0, tiled=True)  55.9 us
    pallas_call x2, Pallas kernels, columns(): pl.pallas_call(columns_kernel, grid=(lats // per_step,), in_specs=[pl.Blo...  54.3 us
    all_to_all x4, starting transfers between devices, exchange(): return lax.all_to_all(values, AXES, split_axis=0, concat_axis=0, tiled=True)  15 us
    pallas_call x1, Pallas kernels, to_spectral(): pl.pallas_call(functools.partial(to_spectral_kernel, per_step), in_specs=...  11.2 us
    ppermute x2, waiting for transfers between devices, sum_over(): lax.ppermute(sent, axis, [(i, i ^ half) for i in range(size)])  9.65 us
    pallas_call x1, Pallas kernels, to_fourier(): pl.pallas_call(functools.partial(to_fourier_kernel, group, per_step), in_...  9.13 us
  transfers between devices with their start and end apart: 6, of which 5 were waited for; matrix products, arithmetic and copies ran while one was open for 2% of the time, Pallas kernels for 29%

profile of v5, /device:TPU:0, one launch (start us, length us, event | category | flops | bytes accessed | tf_op | source)
XLA Modules:
  0.0 244.6 jit_solution(6851391158815212472)
XLA Ops:
  0.6 9.1 %shard_map.120 = (bf16[32,8,32,128]{3,2,1,0:T(8,128)(2,1)S(1)}, bf16[32,8,32,128]{3,2,1,0:T(8,128)(2,1)S(1)}) custom-call(s32[1]{0:T(128)} %bitcast.place_ref, bf16[2,32,64,512]{3,2,1,0:T(8,128)(2,1)} %bitcast.20, bf16[32,512,512]{2,1,0:T(8,128)(2,1)} %leg_ref.3), custom_call_target="tpu_custom_call" | custom-call | flops 2147483648 | bytes 25165824 | tf_op jit(solution)/shard_map/pallas_call | solution.py:91
  9.8 0.0 copy-start
  9.8 55.9 %all_to_all.25 = bf16[32,8,32,128]{3,2,1,0:T(8,128)(2,1)} all-to-all(bf16[32,8,32,128]{3,2,1,0:T(8,128)(2,1)S(1)} %get-tuple-element.17), channel_id=1, replica_groups=mesh['lat'=16,'lev'=2] {'lat','lev'}, dimensions={0} | all-to-all | bytes 4194304 | tf_op jit(solution)/shard_map/all_to_all | solution.py:347
  65.7 0.0 copy-done
  65.7 3.7 %all-to-all-start.2 = ((bf16[32,8,32,128]{3,2,1,0:T(8,128)(2,1)}), bf16[32,8,32,128]{3,2,1,0:T(8,128)(2,1)S(1)}, u32[]{:S(2)}, u32[]{:S(2)}) async-start(bf16[32,8,32,128]{3,2,1,0:T(8,128)(2,1)} %copy-done), calls=%async_computation.2 | async-start | bytes 4194304 | tf_op jit(solution)/shard_map/all_to_all | solution.py:347
  69.4 0.8 dynamic_slice.15
  70.2 0.1 fusion
  70.2 0.8 broadcast_in_dim.10.start_ref
  71.1 27.1 %shard_map.121 = (bf16[16,2,8,32,128]{4,3,2,1,0:T(8,128)(2,1)}, f32[1024,128]{1,0:T(8,128)S(1)}) custom-call(f32[8]{0:T(128)S(1)} %get-tuple-element.31.gauss_ref, bf16[16,2,8,32,128]{4,3,2,1,0:T(8,128)(2,1)} %bitcast.23, bf16[16,1024,128]{2,1,0:T(8,128)(2,1)} %cot_ref.3, bf16[1024,1024]{1,0:T(8,128)(2,1)} %constant.34.clone.basis_ref, ...), custom_call_target="tpu_custom_call" | custom-call | flops 9663676416 | bytes 12582912 | tf_op jit(solution)/shard_map/pallas_call | solution.py:197
  98.2 0.0 copy-start.1
  98.2 0.8 copy-done.1
  99.0 19.1 %all-to-all-done.2 = bf16[32,8,32,128]{3,2,1,0:T(8,128)(2,1)S(1)} async-done(((bf16[32,8,32,128]{3,2,1,0:T(8,128)(2,1)}), bf16[32,8,32,128]{3,2,1,0:T(8,128)(2,1)S(1)}, u32[]{:S(2)}, u32[]{:S(2)}) %all-to-all-start.2) | async-done | bytes 2097184 | tf_op jit(solution)/shard_map/all_to_all | solution.py:347
  118.1 4.0 %all-to-all-start.1 = ((bf16[32,8,32,128]{3,2,1,0:T(8,128)(2,1)}), bf16[32,8,32,128]{3,2,1,0:T(8,128)(2,1)}, u32[]{:S(2)}, u32[]{:S(2)}) async-start(bf16[32,8,32,128]{3,2,1,0:T(8,128)(2,1)} %bitcast.21), calls=%async_computation.1 | async-start | bytes 4194304 | tf_op jit(solution)/shard_map/all_to_all | solution.py:347
  122.1 27.1 %shard_map.122 = (bf16[16,2,8,32,128]{4,3,2,1,0:T(8,128)(2,1)}, f32[1024,128]{1,0:T(8,128)S(1)}) custom-call(f32[8]{0:T(128)S(1)} %get-tuple-element.30.gauss_ref, bf16[16,2,8,32,128]{4,3,2,1,0:T(8,128)(2,1)S(1)} %bitcast.16, bf16[16,1024,128]{2,1,0:T(8,128)(2,1)} %cot_ref.3, bf16[1024,1024]{1,0:T(8,128)(2,1)} %constant.34.clone.basis_ref, ...), custom_call_target="tpu_custom_call" | custom-call | flops 9663676416 | bytes 12582912 | tf_op jit(solution)/shard_map/pallas_call | solution.py:197
  149.3 0.0 copy-start.3
  149.3 1.6 collective-permute-start
  150.9 8.3 %collective-permute-done = f32[1,512,128]{2,1,0:T(8,128)S(1)} collective-permute-done((f32[1,512,128]{2,1,0:T(8,128)S(1)}, f32[1,512,128]{2,1,0:T(8,128)S(1)}, u32[]{:S(2)}, u32[]{:S(2)}) %collective-permute-start) | collective-permute-done | bytes 262176 | tf_op jit(solution)/shard_map/ppermute | solution.py:357
  159.3 0.1 collective-permute-start.1
  159.3 1.3 collective-permute-done.1
  160.7 0.1 convert_element_type.47
  160.8 0.1 subtract_convert_fusion
  160.9 0.3 pad_maximum_fusion.1
  161.2 0.1 reshape.69
  161.3 0.0 copy-done.3
  161.3 1.6 pad_maximum_fusion
  162.9 7.8 %all-to-all-done.1.in_ref = bf16[32,8,32,128]{3,2,1,0:T(8,128)(2,1)} async-done(((bf16[32,8,32,128]{3,2,1,0:T(8,128)(2,1)}), bf16[32,8,32,128]{3,2,1,0:T(8,128)(2,1)}, u32[]{:S(2)}, u32[]{:S(2)}) %all-to-all-start.1) | async-done | bytes 2097184 | tf_op jit(solution)/shard_map/all_to_all | solution.py:347
  170.6 3.7 %all-to-all-start.3 = ((bf16[32,17,16,128]{3,2,1,0:T(8,128)(2,1)}), bf16[32,17,16,128]{3,2,1,0:T(8,128)(2,1)S(1)}, u32[]{:S(2)}, u32[]{:S(2)}) async-start(bf16[32,17,16,128]{3,2,1,0:T(8,128)(2,1)} %pad_maximum_fusion), calls=%async_computation.3 | async-start | bytes 4456448 | tf_op jit(solution)/shard_map/all_to_all | solution.py:347
  174.3 4.5 %shard_map.123.early_ref = bf16[32,32,8,128]{3,2,1,0:T(8,128)(2,1)} custom-call(bf16[32,8,32,128]{3,2,1,0:T(8,128)(2,1)} %all-to-all-done.1.in_ref), custom_call_target="tpu_custom_call" | custom-call | bytes 8388608 | tf_op jit(solution)/shard_map/pallas_call | solution.py:334
  178.8 1.3 slice_bitcast_fusion.after_ref
  180.0 45.8 %all-to-all-done.3.late_ref = bf16[32,17,16,128]{3,2,1,0:T(8,128)(2,1)S(1)} async-done(((bf16[32,17,16,128]{3,2,1,0:T(8,128)(2,1)}), bf16[32,17,16,128]{3,2,1,0:T(8,128)(2,1)S(1)}, u32[]{:S(2)}, u32[]{:S(2)}) %all-to-all-start.3) | async-done | bytes 2228256 | tf_op jit(solution)/shard_map/all_to_all | solution.py:347
  225.9 0.0 copy-start.2
  225.9 0.1 reshape.70
  226.1 0.1 reduce_sum.9
  226.2 1.0 broadcast_in_dim.12
  227.3 3.7 %all-to-all-start.4 = ((bf16[32,32,128]{2,1,0:T(8,128)(2,1)}), bf16[32,32,128]{2,1,0:T(8,128)(2,1)S(1)}, u32[]{:S(2)}, u32[]{:S(2)}) async-start(bf16[32,32,128]{2,1,0:T(8,128)(2,1)} %broadcast_in_dim.12), calls=%async_computation.4 | async-start | bytes 524288 | tf_op jit(solution)/shard_map/all_to_all | solution.py:347
  230.9 0.0 copy-done.2
  230.9 11.2 %shard_map.124 = f32[2,32,64,512]{3,2,1,0:T(8,128)} custom-call(s32[1]{0:T(128)} %bitcast.place_ref, bf16[32,512,512]{2,1,0:T(8,128)(2,1)} %leg_ref.3, bf16[32,32,8,128]{3,2,1,0:T(8,128)(2,1)} %shard_map.123.early_ref, bf16[32,17,16,128]{3,2,1,0:T(8,128)(2,1)} %copy-done.2, bf16[8,128]{1,0:T(8,128)(2,1)} %slice_bitcast_fusion.after_ref), custom_call_target="tpu_custom_call" | custom-call | flops 2147483648 | bytes 29360128 | tf_op jit(solution)/shard_map/pallas_call | solution.py:293
  242.1 0.0 all-to-all-done.4.every_ref
  242.1 0.0 copy-start.4
  242.1 0.7 copy-done.4
  242.8 1.8 shard_map.125
  (8 shorter events, 0.1 us)
Async XLA Ops:
  9.8 55.9 %copy-start = (bf16[32,8,32,128]{3,2,1,0:T(8,128)(2,1)}, bf16[32,8,32,128]{3,2,1,0:T(8,128)(2,1)S(1)}, u32[]{:S(2)}) copy-start(bf16[32,8,32,128]{3,2,1,0:T(8,128)(2,1)S(1)} %get-tuple-element.19) | copy-start | bytes 6291460
  65.7 52.4 %all-to-all-start.2 = ((bf16[32,8,32,128]{3,2,1,0:T(8,128)(2,1)}), bf16[32,8,32,128]{3,2,1,0:T(8,128)(2,1)S(1)}, u32[]{:S(2)}, u32[]{:S(2)}) async-start(bf16[32,8,32,128]{3,2,1,0:T(8,128)(2,1)} %copy-done), calls=%async_computation.2 | async-start | bytes 4194304 | tf_op jit(solution)/shard_map/all_to_all | solution.py:347
  98.2 0.8 copy-start.1
  118.1 52.5 %all-to-all-start.1 = ((bf16[32,8,32,128]{3,2,1,0:T(8,128)(2,1)}), bf16[32,8,32,128]{3,2,1,0:T(8,128)(2,1)}, u32[]{:S(2)}, u32[]{:S(2)}) async-start(bf16[32,8,32,128]{3,2,1,0:T(8,128)(2,1)} %bitcast.21), calls=%async_computation.1 | async-start | bytes 4194304 | tf_op jit(solution)/shard_map/all_to_all | solution.py:347
  149.3 12.0 %copy-start.3 = (bf16[16,2,8,32,128]{4,3,2,1,0:T(8,128)(2,1)S(1)}, bf16[16,2,8,32,128]{4,3,2,1,0:T(8,128)(2,1)}, u32[]{:S(2)}) copy-start(bf16[16,2,8,32,128]{4,3,2,1,0:T(8,128)(2,1)} %get-tuple-element.21) | copy-start | bytes 6291460
  149.3 9.9 %collective-permute-start = (f32[1,512,128]{2,1,0:T(8,128)S(1)}, f32[1,512,128]{2,1,0:T(8,128)S(1)}, u32[]{:S(2)}, u32[]{:S(2)}) collective-permute-start(f32[1,512,128]{2,1,0:T(8,128)S(1)} %constant_dynamic-slice_fusion.1), channel_id=1, source_target_pairs={{0,1},{1,0},{2,3},{3,2},{4,5},{5,4},{6,7},{7,6},{8,9},{9,8},{10,11... | collective-permute-start | bytes 786440 | tf_op jit(solution)/shard_map/ppermute | solution.py:357
  159.3 1.4 collective-permute-start.1
  170.6 55.3 %all-to-all-start.3 = ((bf16[32,17,16,128]{3,2,1,0:T(8,128)(2,1)}), bf16[32,17,16,128]{3,2,1,0:T(8,128)(2,1)S(1)}, u32[]{:S(2)}, u32[]{:S(2)}) async-start(bf16[32,17,16,128]{3,2,1,0:T(8,128)(2,1)} %pad_maximum_fusion), calls=%async_computation.3 | async-start | bytes 4456448 | tf_op jit(solution)/shard_map/all_to_all | solution.py:347
  225.9 5.0 %copy-start.2 = (bf16[32,17,16,128]{3,2,1,0:T(8,128)(2,1)}, bf16[32,17,16,128]{3,2,1,0:T(8,128)(2,1)S(1)}, u32[]{:S(2)}) copy-start(bf16[32,17,16,128]{3,2,1,0:T(8,128)(2,1)S(1)} %all-to-all-done.3.late_ref) | copy-start | bytes 6684676
  227.3 14.9 %all-to-all-start.4 = ((bf16[32,32,128]{2,1,0:T(8,128)(2,1)}), bf16[32,32,128]{2,1,0:T(8,128)(2,1)S(1)}, u32[]{:S(2)}, u32[]{:S(2)}) async-start(bf16[32,32,128]{2,1,0:T(8,128)(2,1)} %broadcast_in_dim.12), calls=%async_computation.4 | async-start | bytes 524288 | tf_op jit(solution)/shard_map/all_to_all | solution.py:347
  242.1 0.7 copy-start.4

commit v6 on v5

--- a/solution.py
+++ b/solution.py
@@ -78,7 +78,7 @@
                 outs[c][pl.ds(p, 1), :, block * group : (block + 1) * group] = rows
             return carry
 
-        lax.fori_loop(0, peers, move, 0)
+        lax.fori_loop(0, peers, move, 0, unroll=4)
 
 
 def to_fourier(place, spec, legendre, peers, chunks):
@@ -260,7 +260,7 @@
         hold[pl.ds(start, chunk_lats * waves), :] = rows.astype(F32)
         return carry
 
-    lax.fori_loop(0, peers, move, 0)
+    lax.fori_loop(0, peers, move, 0, unroll=4)
 
     def work(step, carry):
         for copy in copies(step):
@@ -322,7 +322,7 @@
         hold[pl.ds(start, lats * group), :] = rows.astype(F32)
         return carry
 
-    lax.fori_loop(0, peers, move, 0)
+    lax.fori_loop(0, peers, move, 0, unroll=4)
     for place in range(group):
         rows = hold[pl.ds(place, peers * lats, stride=group), :]
         out_ref[place] = rows.astype(BF16).reshape(peers, lats, width)
@@ -388,7 +388,7 @@
             functools.partial(gradients_kernel, rows),
             out_shape=[jax.ShapeDtypeStruct(shape, F32) for shape in shapes],
             scratch_shapes=[pltpu.VMEM((total, feats), F32)],
-        )(every)
+        )(in_hbm(every))
     flat = jnp.moveaxis(every.astype(F32), 0, 2).reshape(-1, feats)
     first, second = flat[: halves * feats], flat[halves * feats : halves * (feats + hidden)]
     return (

time: 245 us -> 245 us (level)
  no operation moved by 1% of the time
where the time goes in v6:
time: 245 us; the launch traced here: 244 us
  waiting for transfers between devices  82.6 us (34%)
  Pallas kernels  80.4 us (33%)
  blocking collectives  55.9 us (23%)
  starting transfers between devices  16.7 us (7%)
  local copies, waits for them, and re-layouts  5.72 us (2%)
    all_to_all x4, waiting for transfers between devices, exchange(): return lax.all_to_all(values, AXES, split_axis=0, concat_axis=0, tiled=True)  72.9 us
    all_to_all x1, blocking collectives, exchange(): return lax.all_to_all(values, AXES, split_axis=0, concat_axis=0, tiled=True)  55.9 us
    pallas_call x2, Pallas kernels, columns(): pl.pallas_call(columns_kernel, grid=(lats // per_step,), in_specs=[pl.Blo...  54.3 us
    all_to_all x4, starting transfers between devices, exchange(): return lax.all_to_all(values, AXES, split_axis=0, concat_axis=0, tiled=True)  15 us
    pallas_call x1, Pallas kernels, to_spectral(): pl.pallas_call(functools.partial(to_spectral_kernel, per_step), in_specs=...  11.1 us
    ppermute x2, waiting for transfers between devices, sum_over(): lax.ppermute(sent, axis, [(i, i ^ half) for i in range(size)])  9.66 us
    pallas_call x1, Pallas kernels, to_fourier(): pl.pallas_call(functools.partial(to_fourier_kernel, group, per_step), in_...  9 us
  transfers between devices with their start and end apart: 6, of which 5 were waited for; matrix products, arithmetic and copies ran while one was open for 2% of the time, Pallas kernels for 29%

profile of v6, /device:TPU:0, one launch (start us, length us, event | category | flops | bytes accessed | tf_op | source)
XLA Modules:
  0.0 244.4 jit_solution(9209915857161385355)
XLA Ops:
  0.6 9.0 %shard_map.120 = (bf16[32,8,32,128]{3,2,1,0:T(8,128)(2,1)S(1)}, bf16[32,8,32,128]{3,2,1,0:T(8,128)(2,1)S(1)}) custom-call(s32[1]{0:T(128)} %bitcast.place_ref, bf16[2,32,64,512]{3,2,1,0:T(8,128)(2,1)} %bitcast.20, bf16[32,512,512]{2,1,0:T(8,128)(2,1)} %leg_ref.3), custom_call_target="tpu_custom_call" | custom-call | flops 2147483648 | bytes 25165824 | tf_op jit(solution)/shard_map/pallas_call | solution.py:91
  9.6 0.0 copy-start
  9.7 55.9 %all_to_all.25 = bf16[32,8,32,128]{3,2,1,0:T(8,128)(2,1)} all-to-all(bf16[32,8,32,128]{3,2,1,0:T(8,128)(2,1)S(1)} %get-tuple-element.17), channel_id=1, replica_groups=mesh['lat'=16,'lev'=2] {'lat','lev'}, dimensions={0} | all-to-all | bytes 4194304 | tf_op jit(solution)/shard_map/all_to_all | solution.py:347
  65.6 0.0 copy-done
  65.6 3.7 %all-to-all-start.2 = ((bf16[32,8,32,128]{3,2,1,0:T(8,128)(2,1)}), bf16[32,8,32,128]{3,2,1,0:T(8,128)(2,1)S(1)}, u32[]{:S(2)}, u32[]{:S(2)}) async-start(bf16[32,8,32,128]{3,2,1,0:T(8,128)(2,1)} %copy-done), calls=%async_computation.2 | async-start | bytes 4194304 | tf_op jit(solution)/shard_map/all_to_all | solution.py:347
  69.2 0.8 dynamic_slice.15
  70.0 0.1 fusion
  70.1 0.8 broadcast_in_dim.10.start_ref
  70.9 27.1 %shard_map.121 = (bf16[16,2,8,32,128]{4,3,2,1,0:T(8,128)(2,1)}, f32[1024,128]{1,0:T(8,128)S(1)}) custom-call(f32[8]{0:T(128)S(1)} %get-tuple-element.31.gauss_ref, bf16[16,2,8,32,128]{4,3,2,1,0:T(8,128)(2,1)} %bitcast.23, bf16[16,1024,128]{2,1,0:T(8,128)(2,1)} %cot_ref.3, bf16[1024,1024]{1,0:T(8,128)(2,1)} %constant.34.clone.basis_ref, ...), custom_call_target="tpu_custom_call" | custom-call | flops 9663676416 | bytes 12582912 | tf_op jit(solution)/shard_map/pallas_call | solution.py:197
  98.0 0.0 copy-start.1
  98.0 0.8 copy-done.1
  98.8 19.1 %all-to-all-done.2 = bf16[32,8,32,128]{3,2,1,0:T(8,128)(2,1)S(1)} async-done(((bf16[32,8,32,128]{3,2,1,0:T(8,128)(2,1)}), bf16[32,8,32,128]{3,2,1,0:T(8,128)(2,1)S(1)}, u32[]{:S(2)}, u32[]{:S(2)}) %all-to-all-start.2) | async-done | bytes 2097184 | tf_op jit(solution)/shard_map/all_to_all | solution.py:347
  118.0 4.0 %all-to-all-start.1 = ((bf16[32,8,32,128]{3,2,1,0:T(8,128)(2,1)}), bf16[32,8,32,128]{3,2,1,0:T(8,128)(2,1)}, u32[]{:S(2)}, u32[]{:S(2)}) async-start(bf16[32,8,32,128]{3,2,1,0:T(8,128)(2,1)} %bitcast.21), calls=%async_computation.1 | async-start | bytes 4194304 | tf_op jit(solution)/shard_map/all_to_all | solution.py:347
  122.0 27.1 %shard_map.122 = (bf16[16,2,8,32,128]{4,3,2,1,0:T(8,128)(2,1)}, f32[1024,128]{1,0:T(8,128)S(1)}) custom-call(f32[8]{0:T(128)S(1)} %get-tuple-element.30.gauss_ref, bf16[16,2,8,32,128]{4,3,2,1,0:T(8,128)(2,1)S(1)} %bitcast.16, bf16[16,1024,128]{2,1,0:T(8,128)(2,1)} %cot_ref.3, bf16[1024,1024]{1,0:T(8,128)(2,1)} %constant.34.clone.basis_ref, ...), custom_call_target="tpu_custom_call" | custom-call | flops 9663676416 | bytes 12582912 | tf_op jit(solution)/shard_map/pallas_call | solution.py:197
  149.1 0.0 copy-start.3
  149.1 1.6 collective-permute-start
  150.7 8.3 %collective-permute-done = f32[1,512,128]{2,1,0:T(8,128)S(1)} collective-permute-done((f32[1,512,128]{2,1,0:T(8,128)S(1)}, f32[1,512,128]{2,1,0:T(8,128)S(1)}, u32[]{:S(2)}, u32[]{:S(2)}) %collective-permute-start) | collective-permute-done | bytes 262176 | tf_op jit(solution)/shard_map/ppermute | solution.py:357
  159.1 0.1 collective-permute-start.1
  159.2 1.3 collective-permute-done.1
  160.5 0.1 convert_element_type.47
  160.6 0.1 subtract_convert_fusion
  160.7 0.3 pad_maximum_fusion.1
  161.1 0.1 reshape.69
  161.1 0.0 copy-done.3
  161.2 1.6 pad_maximum_fusion
  162.7 7.8 %all-to-all-done.1.in_ref = bf16[32,8,32,128]{3,2,1,0:T(8,128)(2,1)} async-done(((bf16[32,8,32,128]{3,2,1,0:T(8,128)(2,1)}), bf16[32,8,32,128]{3,2,1,0:T(8,128)(2,1)}, u32[]{:S(2)}, u32[]{:S(2)}) %all-to-all-start.1) | async-done | bytes 2097184 | tf_op jit(solution)/shard_map/all_to_all | solution.py:347
  170.5 3.7 %all-to-all-start.3 = ((bf16[32,17,16,128]{3,2,1,0:T(8,128)(2,1)}), bf16[32,17,16,128]{3,2,1,0:T(8,128)(2,1)S(1)}, u32[]{:S(2)}, u32[]{:S(2)}) async-start(bf16[32,17,16,128]{3,2,1,0:T(8,128)(2,1)} %pad_maximum_fusion), calls=%async_computation.3 | async-start | bytes 4456448 | tf_op jit(solution)/shard_map/all_to_all | solution.py:347
  174.2 4.3 %shard_map.123.early_ref = bf16[32,32,8,128]{3,2,1,0:T(8,128)(2,1)} custom-call(bf16[32,8,32,128]{3,2,1,0:T(8,128)(2,1)} %all-to-all-done.1.in_ref), custom_call_target="tpu_custom_call" | custom-call | bytes 8388608 | tf_op jit(solution)/shard_map/pallas_call | solution.py:334
  178.5 1.3 slice_bitcast_fusion.after_ref
  179.7 46.0 %all-to-all-done.3.late_ref = bf16[32,17,16,128]{3,2,1,0:T(8,128)(2,1)S(1)} async-done(((bf16[32,17,16,128]{3,2,1,0:T(8,128)(2,1)}), bf16[32,17,16,128]{3,2,1,0:T(8,128)(2,1)S(1)}, u32[]{:S(2)}, u32[]{:S(2)}) %all-to-all-start.3) | async-done | bytes 2228256 | tf_op jit(solution)/shard_map/all_to_all | solution.py:347
  225.7 0.0 copy-start.2
  225.8 0.1 reshape.70
  225.9 0.1 reduce_sum.9
  226.1 1.0 broadcast_in_dim.12
  227.1 3.7 %all-to-all-start.4 = ((bf16[32,32,128]{2,1,0:T(8,128)(2,1)}), bf16[32,32,128]{2,1,0:T(8,128)(2,1)S(1)}, u32[]{:S(2)}, u32[]{:S(2)}) async-start(bf16[32,32,128]{2,1,0:T(8,128)(2,1)} %broadcast_in_dim.12), calls=%async_computation.4 | async-start | bytes 524288 | tf_op jit(solution)/shard_map/all_to_all | solution.py:347
  230.8 0.0 copy-done.2
  230.8 11.1 %shard_map.124 = f32[2,32,64,512]{3,2,1,0:T(8,128)} custom-call(s32[1]{0:T(128)} %bitcast.place_ref, bf16[32,512,512]{2,1,0:T(8,128)(2,1)} %leg_ref.3, bf16[32,32,8,128]{3,2,1,0:T(8,128)(2,1)} %shard_map.123.early_ref, bf16[32,17,16,128]{3,2,1,0:T(8,128)(2,1)} %copy-done.2, bf16[8,128]{1,0:T(8,128)(2,1)} %slice_bitcast_fusion.after_ref), custom_call_target="tpu_custom_call" | custom-call | flops 2147483648 | bytes 29360128 | tf_op jit(solution)/shard_map/pallas_call | solution.py:293
  241.9 0.0 all-to-all-done.4.every_ref
  241.9 0.0 copy-start.4
  241.9 0.7 copy-done.4
  242.6 1.8 shard_map.125
  (8 shorter events, 0.1 us)
Async XLA Ops:
  9.6 55.9 %copy-start = (bf16[32,8,32,128]{3,2,1,0:T(8,128)(2,1)}, bf16[32,8,32,128]{3,2,1,0:T(8,128)(2,1)S(1)}, u32[]{:S(2)}) copy-start(bf16[32,8,32,128]{3,2,1,0:T(8,128)(2,1)S(1)} %get-tuple-element.19) | copy-start | bytes 6291460
  65.6 52.4 %all-to-all-start.2 = ((bf16[32,8,32,128]{3,2,1,0:T(8,128)(2,1)}), bf16[32,8,32,128]{3,2,1,0:T(8,128)(2,1)S(1)}, u32[]{:S(2)}, u32[]{:S(2)}) async-start(bf16[32,8,32,128]{3,2,1,0:T(8,128)(2,1)} %copy-done), calls=%async_computation.2 | async-start | bytes 4194304 | tf_op jit(solution)/shard_map/all_to_all | solution.py:347
  98.0 0.8 copy-start.1
  118.0 52.5 %all-to-all-start.1 = ((bf16[32,8,32,128]{3,2,1,0:T(8,128)(2,1)}), bf16[32,8,32,128]{3,2,1,0:T(8,128)(2,1)}, u32[]{:S(2)}, u32[]{:S(2)}) async-start(bf16[32,8,32,128]{3,2,1,0:T(8,128)(2,1)} %bitcast.21), calls=%async_computation.1 | async-start | bytes 4194304 | tf_op jit(solution)/shard_map/all_to_all | solution.py:347
  149.1 12.0 %copy-start.3 = (bf16[16,2,8,32,128]{4,3,2,1,0:T(8,128)(2,1)S(1)}, bf16[16,2,8,32,128]{4,3,2,1,0:T(8,128)(2,1)}, u32[]{:S(2)}) copy-start(bf16[16,2,8,32,128]{4,3,2,1,0:T(8,128)(2,1)} %get-tuple-element.21) | copy-start | bytes 6291460
  149.1 9.9 %collective-permute-start = (f32[1,512,128]{2,1,0:T(8,128)S(1)}, f32[1,512,128]{2,1,0:T(8,128)S(1)}, u32[]{:S(2)}, u32[]{:S(2)}) collective-permute-start(f32[1,512,128]{2,1,0:T(8,128)S(1)} %constant_dynamic-slice_fusion.1), channel_id=1, source_target_pairs={{0,1},{1,0},{2,3},{3,2},{4,5},{5,4},{6,7},{7,6},{8,9},{9,8},{10,11... | collective-permute-start | bytes 786440 | tf_op jit(solution)/shard_map/ppermute | solution.py:357
  159.1 1.4 collective-permute-start.1
  170.5 55.3 %all-to-all-start.3 = ((bf16[32,17,16,128]{3,2,1,0:T(8,128)(2,1)}), bf16[32,17,16,128]{3,2,1,0:T(8,128)(2,1)S(1)}, u32[]{:S(2)}, u32[]{:S(2)}) async-start(bf16[32,17,16,128]{3,2,1,0:T(8,128)(2,1)} %pad_maximum_fusion), calls=%async_computation.3 | async-start | bytes 4456448 | tf_op jit(solution)/shard_map/all_to_all | solution.py:347
  225.7 5.0 %copy-start.2 = (bf16[32,17,16,128]{3,2,1,0:T(8,128)(2,1)}, bf16[32,17,16,128]{3,2,1,0:T(8,128)(2,1)S(1)}, u32[]{:S(2)}) copy-start(bf16[32,17,16,128]{3,2,1,0:T(8,128)(2,1)S(1)} %all-to-all-done.3.late_ref) | copy-start | bytes 6684676
  227.1 14.8 %all-to-all-start.4 = ((bf16[32,32,128]{2,1,0:T(8,128)(2,1)}), bf16[32,32,128]{2,1,0:T(8,128)(2,1)S(1)}, u32[]{:S(2)}, u32[]{:S(2)}) async-start(bf16[32,32,128]{2,1,0:T(8,128)(2,1)} %broadcast_in_dim.12), calls=%async_computation.4 | async-start | bytes 524288 | tf_op jit(solution)/shard_map/all_to_all | solution.py:347
  241.9 0.7 copy-start.4
